TPU v7x, 32 devices: a whole 2x2x4 slice. The times are simulated.
32 devices in a mesh: case: 2 (over y), brick: 4 (over z), sect: 2 (over x), slab: 2 (over core).
Axes of the slice: x: 2, y: 2, z: 4, core: 2. Of those that a mesh axis runs over, the one named last changes fastest.
Arguments:
- geometry: bfloat16 [64, 32, 32, 128], P(None, ('case', 'brick'), ('sect', 'slab')), parts along dimension 1, may hold values from -6 to 6
- conv_kernels: bfloat16 [1, 3, 3, 3, 64, 64], replicated, may hold values from -0.15625 to 0.15625
- point_place: float32 [3, 8192], P(None, ('case', 'brick', 'sect', 'slab')), parts along dimension 1, may hold values from 0 to 1
- point_attr: bfloat16 [8192, 64], P(('case', 'brick', 'sect', 'slab')), parts along dimension 0, may hold values from -6 to 6
- destination: int32 [8192, 1], P(('case', 'brick', 'sect', 'slab')), parts along dimension 0, may hold values from 0 to 7; in each aligned block of 256 rows (0 to 255, 256 to 511, ...) at most 40 rows name the same one
- dense_first: bfloat16 [2, 128, 512], replicated, may hold values from -1 to 1
- dense_middle: bfloat16 [2, 3, 512, 512], replicated, may hold values from -0.5 to 0.5
- dense_last: bfloat16 [2, 4, 512], replicated, may hold values from -0.25 to 0.25
Outputs:
- prediction: float32 [4, 10240], P(None, ('case', 'brick', 'sect', 'slab')), parts along dimension 1
There are 2 independent parts, one for each index of `case`. A program takes and returns all parts, laid end to end along the dimension named above; an argument that names none is the same for every part. Nothing has to cross between parts.
Inputs may be any that keep to these rules, and one draw needn't show every extreme that they name: A destination names a brick index and a sect index as brick * 2 + sect; its sect index fixes the point's section. No destination is named by more than 40 of the points of one device, and some device names some destination exactly 40 times.
All inputs are finite; a program needn't handle non-finite values.
Results may differ from a plain program's by a relative error of at most 0.0075.
Values may be sent and summed in bfloat16 or wider, within the bound.
A program may use at most 64 MiB of HBM per device.

v0:
```python
import jax
import jax.numpy as jnp
from jax import lax
from jax.sharding import PartitionSpec as P


def extended(array, sides, width):
    for axis, dim in sides:
        size, length = (lax.axis_size(axis), array.shape[dim])
        up = [(i, (i + 1) % size) for i in range(size - 1)]
        down = [(j, i) for i, j in up]
        last = lax.slice_in_dim(array, length - width, length, axis=dim)
        leading = lax.slice_in_dim(array, 0, width, axis=dim)
        before = lax.ppermute(last, axis, up)
        after = lax.ppermute(leading, axis, down)
        array = jnp.concatenate([before, array, after], axis=dim)
    return array


def convolve(features_now, kernel):
    response = lax.conv_general_dilated(
        features_now[None],
        kernel,
        (1, 1, 1),
        ((0, 0), (0, 0), (1, 1)),
        dimension_numbers=("NCDHW", "DHWIO", "NCDHW"),
        preferred_element_type=jnp.float32,
    )
    return response[0]


def hat(offset):
    return jnp.maximum(0.0, 1.0 - jnp.abs(offset))


def network(table_rows, first_weights, middle_weights, last_weights):
    activity = jax.nn.gelu(
        jnp.dot(table_rows, first_weights, preferred_element_type=jnp.float32), approximate=True
    ).astype(jnp.bfloat16)
    for ordinal in range(middle_weights.shape[0]):
        activity = jax.nn.gelu(
            jnp.dot(activity, middle_weights[ordinal], preferred_element_type=jnp.float32),
            approximate=True,
        ).astype(jnp.bfloat16)
    return lax.dot_general(
        last_weights, activity, (((1,), (1,)), ((), ())), preferred_element_type=jnp.float32
    )


def on_device(
    geometry,
    conv_kernels,
    point_place,
    point_attr,
    destination,
    dense_first,
    dense_middle,
    dense_last,
):
    channels, span_x, span_y, span_z = geometry.shape
    features_now = geometry
    padded = extended(features_now, (("brick", 1), (("sect", "slab"), 2)), 1)
    response = convolve(padded, conv_kernels[0])
    features_now = (
        features_now.astype(jnp.float32) + jax.nn.gelu(response, approximate=True)
    ).astype(jnp.bfloat16)
    latent = extended(features_now, (("brick", 1), (("sect", "slab"), 2)), 1)
    extent_x = latent.shape[1]
    extent_y = latent.shape[2]
    count = point_place.shape[1]
    local_x = point_place[0] * span_x
    local_y = point_place[1] * span_y
    local_z = point_place[2] * span_z
    weight_x = hat(local_x[None, :] - (jnp.arange(extent_x, dtype=jnp.float32) - 0.5)[:, None])
    weight_y = hat(local_y[None, :] - (jnp.arange(extent_y, dtype=jnp.float32) - 0.5)[:, None])
    weight_z = hat(
        local_z[None, :] - (jnp.arange(span_z, dtype=jnp.float32) + 0.5)[:, None]
    ).astype(jnp.bfloat16)
    block_size = min(512, count)
    block_count = count // block_size
    flat_latent = latent.reshape(channels * extent_x * extent_y, span_z)

    def split_blocks(table):
        return table.reshape(table.shape[0], block_count, block_size).transpose(1, 0, 2)

    def sample(pieces):
        part_z, part_x, part_y = pieces
        partial_sum = jnp.dot(flat_latent, part_z, preferred_element_type=jnp.float32).reshape(
            channels, extent_x, extent_y, block_size
        )
        return jnp.einsum(
            "cxyp,xp,yp->pc", partial_sum, part_x, part_y, precision=lax.Precision.HIGHEST
        )

    sampled = lax.map(
        sample, (split_blocks(weight_z), split_blocks(weight_x), split_blocks(weight_y))
    )
    feature = sampled.reshape(count, channels).astype(jnp.bfloat16)
    table_rows = jnp.concatenate([feature, point_attr], axis=1)
    brick_count = lax.axis_size("brick")
    sect_count = lax.axis_size("sect")
    targets_all = brick_count * sect_count
    capacity = 5 * count // (4 * targets_all)
    target = destination[:, 0]
    onehot = (target[:, None] == jnp.arange(targets_all, dtype=jnp.int32)[None, :]).astype(
        jnp.int32
    )
    before = jnp.cumsum(onehot, axis=0) - onehot
    arrival = jnp.sum(before * onehot, axis=1)
    slot_index = target * capacity + arrival
    upper = target % sect_count >= sect_count // 2
    surface_value = network(table_rows, dense_first[0], dense_middle[0], dense_last[0])
    volume_value = network(table_rows, dense_first[1], dense_middle[1], dense_last[1])
    chosen = jnp.where(upper[None, :], volume_value, surface_value)
    outbox = (
        jnp.zeros((chosen.shape[0], targets_all * capacity), jnp.float32)
        .at[:, slot_index]
        .set(chosen)
    )
    prediction = lax.all_to_all(outbox, ("brick", "sect"), split_axis=1, concat_axis=1, tiled=True)
    return prediction


def solution(mesh):
    in_specs = (
        P(None, ("case", "brick"), ("sect", "slab"), None),
        P(),
        P(None, ("case", "brick", "sect", "slab")),
        P(("case", "brick", "sect", "slab"), None),
        P(("case", "brick", "sect", "slab"), None),
        P(),
        P(),
        P(),
    )
    out_specs = P(None, ("case", "brick", "sect", "slab"))
    return jax.shard_map(
        on_device, mesh=mesh, in_specs=in_specs, out_specs=out_specs, check_vma=False
    )
```

profile of v0, /device:TPU:0, one launch (start us, length us, event | category | flops | bytes accessed | tf_op | source)
XLA Modules:
  0.0 85.7 jit_solution(7794228538194470888)
XLA Ops:
  0.0 0.0 copy-start
  0.0 1.1 %fusion.194 = (bf16[64,1,8,128]{3,2,1,0:T(8,128)(2,1)S(1)}, bf16[64,1,8,128]{3,2,1,0:T(8,128)(2,1)S(1)}) fusion(bf16[64,4,8,128]{3,2,1,0:T(8,128)(2,1)} %param.8), kind=kLoop, calls=%fused_computation.208 | loop fusion | bytes 524288 | tf_op jit(solution)/shard_map/slice | solution.py:13
  1.1 4.9 %collective-permute-start = (bf16[64,1,8,128]{3,0,2,1:T(8,128)(2,1)S(1)}, bf16[64,1,8,128]{3,0,2,1:T(8,128)(2,1)S(1)}, u32[]{:S(2)}, u32[]{:S(2)}) collective-permute-start(bf16[64,1,8,128]{3,0,2,1:T(8,128)(2,1)S(1)} %copy.73), channel_id=1, source_target_pairs={{0,4},{4,8},{8,12},{1,5},{5,9},{9,13},{2,6},{6,10},{10,14},{3,7},{... | collective-permute-start | bytes 393224 | tf_op jit(solution)/shard_map/ppermute | solution.py:14
  6.1 1.3 %collective-permute-start.1 = (bf16[64,1,8,128]{3,0,2,1:T(8,128)(2,1)S(1)}, bf16[64,1,8,128]{3,0,2,1:T(8,128)(2,1)S(1)}, u32[]{:S(2)}, u32[]{:S(2)}) collective-permute-start(bf16[64,1,8,128]{3,0,2,1:T(8,128)(2,1)S(1)} %copy.74), channel_id=1, source_target_pairs={{4,0},{8,4},{12,8},{5,1},{9,5},{13,9},{6,2},{10,6},{14,10},{7,3},{... | collective-permute-start | bytes 393224 | tf_op jit(solution)/shard_map/ppermute | solution.py:15
  7.4 0.8 slice_multiply_fusion.2
  8.2 0.7 fusion.158
  8.9 0.1 maximum_bitcast_fusion.1
  9.0 0.1 maximum_bitcast_fusion.2
  9.1 0.6 reduce-window.6
  9.7 0.2 slice_reduce_fusion
  9.9 0.8 fusion.157
  10.7 0.0 collective-permute-done
  10.7 1.3 %constant_dynamic-update-slice_fusion.1 = bf16[64,6,8,128]{3,0,2,1:T(8,128)(2,1)S(1)} fusion(bf16[64,6,8,128]{3,0,2,1:T(8,128)(2,1)S(1)} %constant_dynamic-update-slice_fusion.2, bf16[64,4,8,128]{3,2,1,0:T(8,128)(2,1)} %param.8), kind=kLoop, calls=%fused_computation.156 | loop fusion | bytes 1048576
  12.0 1.0 %collective-permute-done.1 = bf16[64,1,8,128]{3,0,2,1:T(8,128)(2,1)S(1)} collective-permute-done((bf16[64,1,8,128]{3,0,2,1:T(8,128)(2,1)S(1)}, bf16[64,1,8,128]{3,0,2,1:T(8,128)(2,1)S(1)}, u32[]{:S(2)}, u32[]{:S(2)}) %collective-permute-start.1) | collective-permute-done | bytes 131104 | tf_op jit(solution)/shard_map/ppermute | solution.py:15
  13.0 1.3 %collective-permute-start.2 = (bf16[64,6,1,128]{3,0,2,1:T(8,128)(2,1)S(1)}, bf16[64,6,1,128]{3,0,2,1:T(8,128)(2,1)S(1)}, u32[]{:S(2)}, u32[]{:S(2)}) collective-permute-start(bf16[64,6,1,128]{3,0,2,1:T(8,128)(2,1)S(1)} %get-tuple-element.26), channel_id=1, source_target_pairs={{0,1},{1,2},{2,3},{4,5},{5,6},{6,7},{8,9},{9,10},{10,11},{12,13},{... | collective-permute-start | bytes 294920 | tf_op jit(solution)/shard_map/ppermute | solution.py:14
  14.3 1.3 %collective-permute-start.3 = (bf16[64,6,1,128]{3,0,2,1:T(8,128)(2,1)S(1)}, bf16[64,6,1,128]{3,0,2,1:T(8,128)(2,1)S(1)}, u32[]{:S(2)}, u32[]{:S(2)}) collective-permute-start(bf16[64,6,1,128]{3,0,2,1:T(8,128)(2,1)S(1)} %get-tuple-element.28), channel_id=1, source_target_pairs={{1,0},{2,1},{3,2},{5,4},{6,5},{7,6},{9,8},{10,9},{11,10},{13,12},{... | collective-permute-start | bytes 294920 | tf_op jit(solution)/shard_map/ppermute | solution.py:15
  15.6 1.9 %copy.49 = bf16[64,4,8,128]{0,2,3,1:T(8,128)(2,1)} copy(bf16[64,4,8,128]{3,2,1,0:T(8,128)(2,1)S(1)} %copy-done.2) | data formatting | bytes 1048576 | tf_op args[0]
  17.5 0.0 collective-permute-done.2
  17.5 1.7 %collective-permute-done.3 = bf16[64,6,1,128]{3,0,2,1:T(8,128)(2,1)S(1)} collective-permute-done((bf16[64,6,1,128]{3,0,2,1:T(8,128)(2,1)S(1)}, bf16[64,6,1,128]{3,0,2,1:T(8,128)(2,1)S(1)}, u32[]{:S(2)}, u32[]{:S(2)}) %collective-permute-start.3) | collective-permute-done | bytes 98336 | tf_op jit(solution)/shard_map/ppermute | solution.py:15
  19.2 0.1 maximum_bitcast_fusion
  19.3 1.1 %copy.71 = bf16[64,6,10,1,128]{0,4,2,1,3:T(8,128)(2,1)S(1)} copy(bf16[64,6,10,1,128]{4,0,2,1,3:T(8,128)(2,1)S(1)} %maximum_bitcast_fusion) | data formatting | bytes 1966080
  20.5 2.1 %pad.clone = bf16[64,6,10,1,136]{0,4,2,1,3:T(8,128)(2,1)} pad(bf16[64,6,10,1,128]{0,4,2,1,3:T(8,128)(2,1)S(1)} %copy.71, bf16[]{:T(256)} %constant.40), padding=0_0x0_0x0_0x0_0x1_7 | pad | bytes 2027522 | tf_op jit(solution)/shard_map/broadcast_in_dim | solution.py:22
  22.6 3.6 %reshape.81 = bf16[64,6,10,1,8,17]{0,5,4,2,1,3:T(8,128)(2,1)S(1)} reshape(bf16[64,6,10,1,136]{0,4,2,1,3:T(8,128)(2,1)} %pad.clone) | data formatting | bytes 2088960 | tf_op jit(solution)/shard_map/conv_general_dilated | solution.py:21
  26.2 0.0 copy-start.7
  26.2 0.3 copy.55
  26.5 0.1 slice.113
  26.6 0.3 copy-done.7
  26.9 4.5 %fusion.17 = f32[4,8,8,17,64]{4,2,3,1,0:T(8,128)S(1)} fusion(bf16[64,6,10,1,7,2]{0,4,5,2,1,3:T(8,128)(2,1)S(1)} %slice.113, bf16[64,6,10,1,8,17]{0,4,5,2,1,3:T(8,128)(2,1)S(1)} %copy.55, pred[8,17]{0,1:T(8,128)(4,1)S(1)} %copy-done.7, bf16[1,3,3,3,64,64]{5,4,3,2,1,0:T(8,128)(2,1)S(1)} %copy-done), kind=kOutput, calls=%fused_computation.22 | convolution fusion | flops 966373376 | bytes 2487432 | tf_op jit(solution)/shard_map/conv_general_dilated | solution.py:21
  31.4 0.4 copy.56
  31.8 0.8 copy-done.1
  32.6 0.8 fusion.16
  33.5 3.6 %collective-permute-start.4 = (bf16[64,1,8,128]{0,2,3,1:T(8,128)(2,1)S(1)}, bf16[64,1,8,128]{0,2,3,1:T(8,128)(2,1)S(1)}, u32[]{:S(2)}, u32[]{:S(2)}) collective-permute-start(bf16[64,1,8,128]{0,2,3,1:T(8,128)(2,1)S(1)} %get-tuple-element.17), channel_id=1, source_target_pairs={{0,4},{4,8},{8,12},{1,5},{5,9},{9,13},{2,6},{6,10},{10,14},{3,7},{... | collective-permute-start | bytes 393224 | tf_op jit(solution)/shard_map/ppermute | solution.py:14
  37.1 1.3 %collective-permute-start.5 = (bf16[64,1,8,128]{0,2,3,1:T(8,128)(2,1)S(1)}, bf16[64,1,8,128]{0,2,3,1:T(8,128)(2,1)S(1)}, u32[]{:S(2)}, u32[]{:S(2)}) collective-permute-start(bf16[64,1,8,128]{0,2,3,1:T(8,128)(2,1)S(1)} %get-tuple-element.24), channel_id=1, source_target_pairs={{4,0},{8,4},{12,8},{5,1},{9,5},{13,9},{6,2},{10,6},{14,10},{7,3},{... | collective-permute-start | bytes 393224 | tf_op jit(solution)/shard_map/ppermute | solution.py:15
  38.4 3.0 %collective-permute-done.4 = bf16[64,1,8,128]{0,2,3,1:T(8,128)(2,1)S(1)} collective-permute-done((bf16[64,1,8,128]{0,2,3,1:T(8,128)(2,1)S(1)}, bf16[64,1,8,128]{0,2,3,1:T(8,128)(2,1)S(1)}, u32[]{:S(2)}, u32[]{:S(2)}) %collective-permute-start.4) | collective-permute-done | bytes 131104 | tf_op jit(solution)/shard_map/ppermute | solution.py:14
  41.4 4.7 %collective-permute-done.5 = bf16[64,1,8,128]{0,2,3,1:T(8,128)(2,1)S(1)} collective-permute-done((bf16[64,1,8,128]{0,2,3,1:T(8,128)(2,1)S(1)}, bf16[64,1,8,128]{0,2,3,1:T(8,128)(2,1)S(1)}, u32[]{:S(2)}, u32[]{:S(2)}) %collective-permute-start.5) | collective-permute-done | bytes 131104 | tf_op jit(solution)/shard_map/ppermute | solution.py:15
  46.1 0.4 pad_maximum_fusion
  46.5 1.3 %fusion.191 = (bf16[64,6,1,128]{0,2,3,1:T(2,128)(2,1)}, bf16[64,6,1,128]{0,2,3,1:T(2,128)(2,1)S(1)}) fusion(bf16[64,6,8,128]{0,2,3,1:T(8,128)(2,1)S(1)} %pad_maximum_fusion), kind=kLoop, calls=%fused_computation.205 | loop fusion | bytes 393216 | tf_op jit(solution)/shard_map/slice | solution.py:12
  47.7 4.5 %collective-permute-start.6 = (bf16[64,6,1,128]{0,2,3,1:T(2,128)(2,1)}, bf16[64,6,1,128]{0,2,3,1:T(2,128)(2,1)}, u32[]{:S(2)}, u32[]{:S(2)}) collective-permute-start(bf16[64,6,1,128]{0,2,3,1:T(2,128)(2,1)} %get-tuple-element.15), channel_id=1, source_target_pairs={{0,1},{1,2},{2,3},{4,5},{5,6},{6,7},{8,9},{9,10},{10,11},{12,13},{... | collective-permute-start | bytes 294920 | tf_op jit(solution)/shard_map/ppermute | solution.py:14
  52.2 1.5 %collective-permute-start.7 = (bf16[64,6,1,128]{0,2,3,1:T(2,128)(2,1)S(1)}, bf16[64,6,1,128]{0,2,3,1:T(2,128)(2,1)}, u32[]{:S(2)}, u32[]{:S(2)}) collective-permute-start(bf16[64,6,1,128]{0,2,3,1:T(2,128)(2,1)S(1)} %get-tuple-element.16), channel_id=1, source_target_pairs={{1,0},{2,1},{3,2},{5,4},{6,5},{7,6},{9,8},{10,9},{11,10},{13,12},{... | collective-permute-start | bytes 294920 | tf_op jit(solution)/shard_map/ppermute | solution.py:15
  53.7 1.0 %copy.58 = bf16[64,6,8,128]{3,0,2,1:T(8,128)(2,1)S(1)} copy(bf16[64,6,8,128]{0,2,3,1:T(8,128)(2,1)S(1)} %pad_maximum_fusion) | data formatting | bytes 1572864 | tf_op jit(solution)/shard_map/concatenate | solution.py:16
  54.7 0.0 collective-permute-done.6
  54.7 1.2 %copy.57 = bf16[64,6,1,128]{3,0,2,1:T(8,128)(2,1)S(1)} copy(bf16[64,6,1,128]{0,2,3,1:T(2,128)(2,1)} %collective-permute-done.6) | data formatting | bytes 196608 | tf_op jit(solution)/shard_map/ppermute | solution.py:14
  55.9 0.1 collective-permute-done.7
  56.0 1.2 %copy.59 = bf16[64,6,1,128]{3,0,2,1:T(8,128)(2,1)S(1)} copy(bf16[64,6,1,128]{0,2,3,1:T(2,128)(2,1)} %collective-permute-done.7) | data formatting | bytes 196608 | tf_op jit(solution)/shard_map/ppermute | solution.py:15
  57.2 0.0 copy-start.4
  57.2 0.0 copy-start.5
  57.2 0.9 %multiply_reduce_fusion = bf16[256,64]{0,1:T(8,128)(2,1)S(1)} fusion(f32[256,6,10]{0,2,1:T(8,128)S(1)} %copy.70, bf16[64,6,1,128]{3,0,2,1:T(8,128)(2,1)S(1)} %copy.59, bf16[64,6,8,128]{3,0,2,1:T(8,128)(2,1)S(1)} %copy.58, bf16[64,6,1,128]{3,0,2,1:T(8,128)(2,1)S(1)} %copy.57, f32[128]{0:T(128)S(1)} %iota_add_fusion.2, f32[256]{0:T(256)S(1)} %bitcast.113), kind=kOutput, calls=%fused_computation.3 | convolution fusion | flops 254754816 | bytes 1078784 | tf_op jit(solution)/shard_map/while/body/eval_jaxpr/dot_general | solution.py:88
  58.1 0.1 copy-done.4
  58.1 1.7 %fusion.42 = bf16[256,512]{1,0:T(8,128)(2,1)S(1)} fusion(bf16[2,3,512,512]{3,2,1,0:T(8,128)(2,1)} %param.14, bf16[2,128,512]{2,1,0:T(8,128)(2,1)S(1)} %copy-done.4, bf16[256,64]{0,1:T(8,128)(2,1)S(1)} %copy-done.5, bf16[256,64]{0,1:T(8,128)(2,1)S(1)} %multiply_reduce_fusion), kind=kOutput, calls=%fused_computation.55 | convolution fusion | flops 170262528 | bytes 983040 | tf_op jit(solution)/shard_map/dot_general | solution.py:42
  59.8 1.7 %fusion.75 = bf16[256,512]{1,0:T(8,128)(2,1)S(1)} fusion(bf16[2,3,512,512]{3,2,1,0:T(8,128)(2,1)} %param.14, bf16[2,128,512]{2,1,0:T(8,128)(2,1)S(1)} %copy-done.4, bf16[256,64]{0,1:T(8,128)(2,1)S(1)} %copy-done.5, bf16[256,64]{0,1:T(8,128)(2,1)S(1)} %multiply_reduce_fusion), kind=kOutput, calls=%fused_computation.88 | convolution fusion | flops 170262528 | bytes 983040 | tf_op jit(solution)/shard_map/dot_general | solution.py:42
  61.5 0.0 copy-start.6
  61.5 1.4 %fusion.50 = bf16[256,512]{1,0:T(8,128)(2,1)S(1)} fusion(bf16[256,512]{1,0:T(8,128)(2,1)S(1)} %fusion.42, bf16[2,3,512,512]{3,2,1,0:T(8,128)(2,1)} %param.14), kind=kOutput, calls=%fused_computation.63 | convolution fusion | flops 135397376 | bytes 1048576 | tf_op jit(solution)/shard_map/dot_general | solution.py:42
  63.0 1.4 %fusion.83 = bf16[256,512]{1,0:T(8,128)(2,1)S(1)} fusion(bf16[256,512]{1,0:T(8,128)(2,1)S(1)} %fusion.75, bf16[2,3,512,512]{3,2,1,0:T(8,128)(2,1)} %param.14), kind=kOutput, calls=%fused_computation.96 | convolution fusion | flops 135397376 | bytes 1048576 | tf_op jit(solution)/shard_map/dot_general | solution.py:42
  64.4 1.6 %fusion.108 = f32[256,4]{0,1:T(4,128)S(1)} fusion(bf16[256,512]{1,0:T(8,128)(2,1)S(1)} %fusion.50, bf16[2,3,512,512]{3,2,1,0:T(8,128)(2,1)} %param.14, bf16[2,4,512]{2,1,0:T(4,128)(2,1)S(1)} %copy-done.6), kind=kOutput, calls=%fused_computation.112 | convolution fusion | flops 136445952 | bytes 794624 | tf_op jit(solution)/shard_map/dot_general | solution.py:45
  66.0 1.6 %convolution_select_fusion = f32[256,4]{0,1:T(4,128)S(1)} fusion(f32[256,4]{0,1:T(4,128)S(1)} %fusion.108, bf16[256,512]{1,0:T(8,128)(2,1)S(1)} %fusion.83, bf16[2,3,512,512]{3,2,1,0:T(8,128)(2,1)} %param.14, bf16[2,4,512]{2,1,0:T(4,128)(2,1)S(1)} %copy-done.6, pred[256]{0:T(512)(128)(4,1)S(1)} %fusion.164), kind=kOutput, calls=%fused_computation.24 | convolution fusion | flops 136446976 | bytes 799232 | tf_op jit(solution)/shard_map/dot_general | solution.py:45
  67.6 0.1 copy.60
  67.7 1.2 %scatter_custom_fusion = f32[4,320]{0,1:T(8,128)S(1)} fusion(s32[256]{0:T(256)S(1)} %bitcast.112, f32[256,4]{1,0:T(8,128)S(1)} %copy.60, f32[]{:T(128)} %constant.19.clone.1), kind=kCustom, calls=%fused_computation.145 | custom fusion | bytes 5124 | tf_op jit(solution)/shard_map/scatter | solution.py:118
  68.9 0.1 copy.61
  69.0 0.1 reshape.105
  69.1 14.6 %all_to_all.12 = f32[8,1,160]{2,1,0:T(1,128)S(1)} all-to-all(f32[8,1,160]{2,1,0:T(1,128)S(1)} %reshape.105), channel_id=1, replica_groups=mesh['case'=2,'brick'=4,'sect'=2,'slab'=2] {'brick','sect'}, dimensions={0} | all-to-all | bytes 10240 | tf_op jit(solution)/shard_map/all_to_all | solution.py:120
  83.7 0.5 broadcast.188
  84.2 0.7 reduce.4
  84.9 0.1 reshape.106
  85.0 0.7 all_to_all.10
  (24 shorter events, 0.3 us)
Async XLA Ops:
  0.0 26.6 %copy-start = (bf16[1,3,3,3,64,64]{5,4,3,2,1,0:T(8,128)(2,1)S(1)}, bf16[1,3,3,3,64,64]{5,4,3,2,1,0:T(8,128)(2,1)}, u32[]{:S(2)}) copy-start(bf16[1,3,3,3,64,64]{5,4,3,2,1,0:T(8,128)(2,1)} %param.9) | copy-start | bytes 663556
  0.0 15.6 %copy-start.2 = (bf16[64,4,8,128]{3,2,1,0:T(8,128)(2,1)S(1)}, bf16[64,4,8,128]{3,2,1,0:T(8,128)(2,1)}, u32[]{:S(2)}) copy-start(bf16[64,4,8,128]{3,2,1,0:T(8,128)(2,1)} %param.8) | copy-start | bytes 1572868
  0.0 15.6 %copy-start.3 = (s32[256,1]{0,1:T(1,128)S(1)}, s32[256,1]{0,1:T(1,128)}, u32[]{:S(2)}) copy-start(s32[256,1]{0,1:T(1,128)} %param.12) | copy-start | bytes 3076
  1.1 9.6 %collective-permute-start = (bf16[64,1,8,128]{3,0,2,1:T(8,128)(2,1)S(1)}, bf16[64,1,8,128]{3,0,2,1:T(8,128)(2,1)S(1)}, u32[]{:S(2)}, u32[]{:S(2)}) collective-permute-start(bf16[64,1,8,128]{3,0,2,1:T(8,128)(2,1)S(1)} %copy.73), channel_id=1, source_target_pairs={{0,4},{4,8},{8,12},{1,5},{5,9},{9,13},{2,6},{6,10},{10,14},{3,7},{... | collective-permute-start | bytes 393224 | tf_op jit(solution)/shard_map/ppermute | solution.py:14
  6.1 6.9 %collective-permute-start.1 = (bf16[64,1,8,128]{3,0,2,1:T(8,128)(2,1)S(1)}, bf16[64,1,8,128]{3,0,2,1:T(8,128)(2,1)S(1)}, u32[]{:S(2)}, u32[]{:S(2)}) collective-permute-start(bf16[64,1,8,128]{3,0,2,1:T(8,128)(2,1)S(1)} %copy.74), channel_id=1, source_target_pairs={{4,0},{8,4},{12,8},{5,1},{9,5},{13,9},{6,2},{10,6},{14,10},{7,3},{... | collective-permute-start | bytes 393224 | tf_op jit(solution)/shard_map/ppermute | solution.py:15
  13.0 4.5 %collective-permute-start.2 = (bf16[64,6,1,128]{3,0,2,1:T(8,128)(2,1)S(1)}, bf16[64,6,1,128]{3,0,2,1:T(8,128)(2,1)S(1)}, u32[]{:S(2)}, u32[]{:S(2)}) collective-permute-start(bf16[64,6,1,128]{3,0,2,1:T(8,128)(2,1)S(1)} %get-tuple-element.26), channel_id=1, source_target_pairs={{0,1},{1,2},{2,3},{4,5},{5,6},{6,7},{8,9},{9,10},{10,11},{12,13},{... | collective-permute-start | bytes 294920 | tf_op jit(solution)/shard_map/ppermute | solution.py:14
  14.3 4.9 %collective-permute-start.3 = (bf16[64,6,1,128]{3,0,2,1:T(8,128)(2,1)S(1)}, bf16[64,6,1,128]{3,0,2,1:T(8,128)(2,1)S(1)}, u32[]{:S(2)}, u32[]{:S(2)}) collective-permute-start(bf16[64,6,1,128]{3,0,2,1:T(8,128)(2,1)S(1)} %get-tuple-element.28), channel_id=1, source_target_pairs={{1,0},{2,1},{3,2},{5,4},{6,5},{7,6},{9,8},{10,9},{11,10},{13,12},{... | collective-permute-start | bytes 294920 | tf_op jit(solution)/shard_map/ppermute | solution.py:15
  26.2 0.7 copy-start.7
  31.4 1.2 %copy-start.1 = (bf16[64,4,8,128]{0,2,3,1:T(8,128)(2,1)S(1)}, bf16[64,4,8,128]{0,2,3,1:T(8,128)(2,1)}, u32[]{:S(2)}) copy-start(bf16[64,4,8,128]{0,2,3,1:T(8,128)(2,1)} %copy.49) | copy-start | bytes 1572868
  33.5 8.0 %collective-permute-start.4 = (bf16[64,1,8,128]{0,2,3,1:T(8,128)(2,1)S(1)}, bf16[64,1,8,128]{0,2,3,1:T(8,128)(2,1)S(1)}, u32[]{:S(2)}, u32[]{:S(2)}) collective-permute-start(bf16[64,1,8,128]{0,2,3,1:T(8,128)(2,1)S(1)} %get-tuple-element.17), channel_id=1, source_target_pairs={{0,4},{4,8},{8,12},{1,5},{5,9},{9,13},{2,6},{6,10},{10,14},{3,7},{... | collective-permute-start | bytes 393224 | tf_op jit(solution)/shard_map/ppermute | solution.py:14
  37.1 9.0 %collective-permute-start.5 = (bf16[64,1,8,128]{0,2,3,1:T(8,128)(2,1)S(1)}, bf16[64,1,8,128]{0,2,3,1:T(8,128)(2,1)S(1)}, u32[]{:S(2)}, u32[]{:S(2)}) collective-permute-start(bf16[64,1,8,128]{0,2,3,1:T(8,128)(2,1)S(1)} %get-tuple-element.24), channel_id=1, source_target_pairs={{4,0},{8,4},{12,8},{5,1},{9,5},{13,9},{6,2},{10,6},{14,10},{7,3},{... | collective-permute-start | bytes 393224 | tf_op jit(solution)/shard_map/ppermute | solution.py:15
  47.7 7.0 %collective-permute-start.6 = (bf16[64,6,1,128]{0,2,3,1:T(2,128)(2,1)}, bf16[64,6,1,128]{0,2,3,1:T(2,128)(2,1)}, u32[]{:S(2)}, u32[]{:S(2)}) collective-permute-start(bf16[64,6,1,128]{0,2,3,1:T(2,128)(2,1)} %get-tuple-element.15), channel_id=1, source_target_pairs={{0,1},{1,2},{2,3},{4,5},{5,6},{6,7},{8,9},{9,10},{10,11},{12,13},{... | collective-permute-start | bytes 294920 | tf_op jit(solution)/shard_map/ppermute | solution.py:14
  52.2 3.7 %collective-permute-start.7 = (bf16[64,6,1,128]{0,2,3,1:T(2,128)(2,1)S(1)}, bf16[64,6,1,128]{0,2,3,1:T(2,128)(2,1)}, u32[]{:S(2)}, u32[]{:S(2)}) collective-permute-start(bf16[64,6,1,128]{0,2,3,1:T(2,128)(2,1)S(1)} %get-tuple-element.16), channel_id=1, source_target_pairs={{1,0},{2,1},{3,2},{5,4},{6,5},{7,6},{9,8},{10,9},{11,10},{13,12},{... | collective-permute-start | bytes 294920 | tf_op jit(solution)/shard_map/ppermute | solution.py:15
  57.2 1.0 %copy-start.4 = (bf16[2,128,512]{2,1,0:T(8,128)(2,1)S(1)}, bf16[2,128,512]{2,1,0:T(8,128)(2,1)}, u32[]{:S(2)}) copy-start(bf16[2,128,512]{2,1,0:T(8,128)(2,1)} %param.13) | copy-start | bytes 786436
  57.2 0.9 %copy-start.5 = (bf16[256,64]{0,1:T(8,128)(2,1)S(1)}, bf16[256,64]{0,1:T(8,128)(2,1)}, u32[]{:S(2)}) copy-start(bf16[256,64]{0,1:T(8,128)(2,1)} %param.11) | copy-start | bytes 98308
  61.5 2.9 %copy-start.6 = (bf16[2,4,512]{2,1,0:T(4,128)(2,1)S(1)}, bf16[2,4,512]{2,1,0:T(4,128)(2,1)}, u32[]{:S(2)}) copy-start(bf16[2,4,512]{2,1,0:T(4,128)(2,1)} %param.15) | copy-start | bytes 24580
where the time goes:
time: 86.6 us; the launch traced here: 85.7 us
  local copies, waits for them, and re-layouts  20.8 us (24%)
  starting transfers between devices  19.7 us (23%)
  matrix products  14.8 us (17%)
  blocking collectives  14.6 us (17%)
  waiting for transfers between devices  10.4 us (12%)
  other arithmetic  5.07 us (6%)
    all_to_all x1, blocking collectives, on_device(): lax.all_to_all(outbox, ('brick', 'sect'), split_axis=1, concat_axis=1, ti...  14.6 us
    ppermute x4, starting transfers between devices, extended(): before = lax.ppermute(last, axis, up)  14.4 us
    ppermute x4, waiting for transfers between devices, extended(): after = lax.ppermute(leading, axis, down)  7.42 us
    dot_general x4, matrix products, network(): jnp.dot(activity, middle_weights[ordinal], preferred_element_type=jnp.flo...  6.27 us
    unnamed x25, local copies, waits for them, and re-layouts  5.7 us
    ppermute x4, starting transfers between devices, extended(): after = lax.ppermute(leading, axis, down)  5.34 us
    conv_general_dilated x1, matrix products, convolve(): lax.conv_general_dilated(features_now[None], kernel, (1, 1, 1), ((0, 0),...  4.51 us
    conv_general_dilated x4, local copies, waits for them, and re-layouts, convolve(): lax.conv_general_dilated(features_now[None], kernel, (1, 1, 1), ((0, 0),...  4.4 us
  transfers between devices with their start and end apart: 8, of which 5 were waited for; matrix products, arithmetic and copies ran while one was open for 10% of the time, Pallas kernels for 0%

commit v1 on v0

v1 whole, which is shorter than its diff:
```python
import functools

import jax
import jax.numpy as jnp
from jax import lax
from jax.experimental import pallas as pl
from jax.experimental.pallas import tpu as pltpu
from jax.sharding import PartitionSpec as P

MESH = pl.DeviceIdType.MESH
DIRECTIONS = ((1, 0), (-1, 0), (1, 1), (1, -1), (-1, 1), (-1, -1), (0, 1), (0, -1))
NT = (((1,), (1,)), ((), ()))


def hat(offset):
    return jnp.maximum(0.0, 1.0 - jnp.abs(offset))


def gelu(value):
    return jax.nn.gelu(value, approximate=True)


def dot(a, b):
    return jnp.dot(a, b, preferred_element_type=jnp.float32)


def send_range(step, size):
    return {1: pl.ds(size, 1), -1: pl.ds(1, 1), 0: pl.ds(1, size)}[step]


def land_range(step, size):
    return {1: pl.ds(0, 1), -1: pl.ds(size + 1, 1), 0: pl.ds(1, size)}[step]


def kernel(
    bricks,
    sects,
    slabs,
    geometry,
    kernels,
    place,
    attr,
    target,
    first,
    middle,
    last,
    out,
    geo,
    wide,
    pad,
    lat,
    taps,
    taps_t,
    first_v,
    middle_v,
    outbox,
    inbox,
    local_sem,
    send_sem,
    recv_sem,
    value_send,
    value_recv,
):
    channels, span_x, span_y, span_z = geo.shape
    count = place.shape[1]
    peers = bricks * sects
    cap = 5 * count // (4 * peers)
    half = peers // 2 * cap
    brick = lax.axis_index("brick")
    sect = lax.axis_index("sect")
    slab = lax.axis_index("slab")
    column = sect * slabs + slab
    columns = sects * slabs
    me = brick * sects + sect
    linear = me * slabs + slab
    everyone = peers * slabs

    barrier = pltpu.get_barrier_semaphore()
    for j in range(1, everyone):
        other = lax.rem(linear + j, everyone)
        pl.semaphore_signal(
            barrier,
            inc=1,
            device_id={
                "brick": other // columns,
                "sect": other % columns // slabs,
                "slab": other % slabs,
            },
            device_id_type=MESH,
        )

    loads = [
        pltpu.make_async_copy(geometry, geo, local_sem.at[0]),
        pltpu.make_async_copy(kernels, taps, local_sem.at[1]),
        pltpu.make_async_copy(first, first_v, local_sem.at[2]),
        pltpu.make_async_copy(middle, middle_v, local_sem.at[3]),
    ]
    for load in loads:
        load.start()

    loads[0].wait()
    for x in range(span_x):
        wide[...] = geo[:, x].astype(jnp.float32).reshape(channels * span_y, span_z)
        for y in range(span_y):
            pad[x + 1, y + 1] = wide[pl.ds(y, channels, stride=span_y), :].astype(jnp.bfloat16)

    def inside(dx, dy):
        b, c = brick + dx, column + dy
        return (b >= 0) & (b < bricks) & (c >= 0) & (c < columns)

    def halo_copy(buffer, phase, k):
        dx, dy = DIRECTIONS[k]
        c = column + dy
        return pltpu.make_async_remote_copy(
            src_ref=buffer.at[send_range(dx, span_x), send_range(dy, span_y)],
            dst_ref=buffer.at[land_range(dx, span_x), land_range(dy, span_y)],
            send_sem=send_sem.at[phase, k],
            recv_sem=recv_sem.at[phase, k],
            device_id={"brick": brick + dx, "sect": c // slabs, "slab": c % slabs},
            device_id_type=MESH,
        )

    def start(buffer, phase, which):
        for k in which:
            @pl.when(inside(*DIRECTIONS[k]))
            def _():
                halo_copy(buffer, phase, k).start()

    def land(buffer, phase, which):
        for k in which:
            dx, dy = DIRECTIONS[k]

            @pl.when(inside(-dx, -dy))
            def _():
                halo_copy(buffer, phase, k).wait_recv()

    def drain(buffer, phase):
        for k in range(8):
            @pl.when(inside(*DIRECTIONS[k]))
            def _():
                halo_copy(buffer, phase, k).wait_send()

    pl.semaphore_wait(barrier, everyone - 1)
    start(pad, 0, range(8))

    for k, (dx, dy) in enumerate(DIRECTIONS):
        @pl.when(jnp.logical_not(inside(-dx, -dy)))
        def _():
            for buffer in (pad, lat):
                region = buffer.at[land_range(dx, span_x), land_range(dy, span_y)]
                region[...] = jnp.zeros(region.shape, jnp.bfloat16)

    loads[1].wait()
    for a in range(3):
        for b in range(3):
            for e in range(3):
                tap = taps[0, a, b, e].astype(jnp.float32).T.astype(jnp.bfloat16)
                taps_t[a, e * channels:(e + 1) * channels, b * channels:(b + 1) * channels] = tap

    local_x = place[0:1, :] * span_x
    local_y = place[1:2, :] * span_y
    local_z = place[2:3, :] * span_z
    cells = lax.broadcasted_iota(jnp.int32, (span_z, count), 0).astype(jnp.float32)
    weight_z = hat(local_z - (cells + 0.5)).astype(jnp.bfloat16)
    weight_x = [hat(local_x - (x - 0.5)) for x in range(span_x + 2)]
    weight_y = [hat(local_y - (y - 0.5)) for y in range(span_y + 2)]

    named = lax.broadcasted_iota(jnp.int32, (peers, count), 0)
    onehot = named == target[...]
    earlier = lax.broadcasted_iota(jnp.int32, (count, count), 0) < lax.broadcasted_iota(
        jnp.int32, (count, count), 1
    )
    before = dot(onehot.astype(jnp.bfloat16), earlier.astype(jnp.bfloat16))
    named_brick = lax.div(named, jnp.int32(sects))
    named_sect = named - named_brick * sects
    upper = (named_sect >= sects // 2).astype(jnp.int32)
    block = upper * (peers // 2) + named_brick * (sects // 2) + named_sect - upper * (sects // 2)
    position = jnp.sum(
        jnp.where(onehot, before + (block * cap).astype(jnp.float32), 0.0), axis=0, keepdims=True
    )
    slots = lax.broadcasted_iota(jnp.int32, (2 * half, count), 0)
    gather = (slots == position.astype(jnp.int32)).astype(jnp.bfloat16)

    lane = lax.broadcasted_iota(jnp.int32, (channels, span_z), 1)

    def conv_row(x):
        total = None
        for a in range(3):
            near = jnp.concatenate(
                [pad[x + a, y:y + 3].reshape(3 * channels, span_z) for y in range(span_y)], axis=1
            )
            term = dot(taps_t[a], near)
            total = term if total is None else total + term
        for y in range(span_y):
            part = total[:, y * span_z:(y + 1) * span_z]
            left = pltpu.roll(part[:channels], 1, 1)
            right = pltpu.roll(part[2 * channels:], span_z - 1, 1)
            response = (
                part[channels:2 * channels]
                + jnp.where(lane == 0, 0.0, left)
                + jnp.where(lane == span_z - 1, 0.0, right)
            )
            old = pad[x + 1, y + 1].astype(jnp.float32)
            lat[x + 1, y + 1] = (old + gelu(response)).astype(jnp.bfloat16)

    land(pad, 0, (6, 7))
    for x in range(1, span_x - 1):
        conv_row(x)
    land(pad, 0, range(6))
    conv_row(0)
    conv_row(span_x - 1)
    start(lat, 1, range(8))

    def sample(total, x, low, high):
        part = dot(lat[x, low:high].reshape((high - low) * channels, span_z), weight_z)
        inner = None
        for y in range(low, high):
            term = part[(y - low) * channels:(y - low + 1) * channels] * weight_y[y]
            inner = term if inner is None else inner + term
        inner = inner * weight_x[x]
        return inner if total is None else total + inner

    total = None
    for x in range(1, span_x + 1):
        total = sample(total, x, 1, span_y + 1)
    land(lat, 1, (6, 7))
    for x in range(1, span_x + 1):
        total = sample(total, x, 0, 1)
        total = sample(total, x, span_y + 1, span_y + 2)
    land(lat, 1, range(6))
    for x in (0, span_x + 1):
        total = sample(total, x, 0, span_y + 2)
    row = jnp.concatenate([total.astype(jnp.bfloat16), attr[...]], axis=0)
    table = lax.dot_general(gather, row, NT, preferred_element_type=jnp.float32)
    table = table.astype(jnp.bfloat16)

    loads[2].wait()
    loads[3].wait()
    outbox[...] = jnp.zeros(outbox.shape, jnp.float32)
    for s in range(2):
        act = gelu(dot(table[s * half:(s + 1) * half], first_v[s])).astype(jnp.bfloat16)
        for layer in range(middle.shape[1]):
            act = gelu(dot(act, middle_v[s, layer])).astype(jnp.bfloat16)
        value = lax.dot_general(last[s], act, NT, preferred_element_type=jnp.float32)
        outbox[s, 0:value.shape[0], 0:half] = value

    def value_copy(j):
        other = lax.rem(me + j, peers)
        there = other % sects
        return pltpu.make_async_remote_copy(
            src_ref=outbox.at[there // (sects // 2)],
            dst_ref=inbox.at[me],
            send_sem=value_send.at[j],
            recv_sem=value_recv.at[j],
            device_id={"brick": other // sects, "sect": there},
            device_id_type=MESH,
        )

    for j in range(1, peers):
        value_copy(j).start()
    inbox[me] = outbox[sect // (sects // 2)]
    drain(pad, 0)
    drain(lat, 1)
    for j in range(1, peers):
        value_copy(j).wait()

    width = inbox.shape[2]
    own = (brick * (sects // 2) + sect % (sects // 2)) * cap
    rolled = pltpu.roll(inbox[...].reshape(peers * 8, width), lax.rem(width - own, width), 1)
    for i in range(peers):
        out[:, i * cap:(i + 1) * cap] = rolled[i * 8:i * 8 + out.shape[0], 0:cap]


def on_device(
    sizes,
    geometry,
    conv_kernels,
    point_place,
    point_attr,
    destination,
    dense_first,
    dense_middle,
    dense_last,
):
    bricks, sects, slabs = sizes
    channels, span_x, span_y, span_z = geometry.shape
    count = point_place.shape[1]
    peers = bricks * sects
    cap = 5 * count // (4 * peers)
    width = -(-(peers // 2 * cap) // 128) * 128
    padded = (span_x + 2, span_y + 2, channels, span_z)
    anywhere = pl.BlockSpec(memory_space=pl.ANY)
    local = pl.BlockSpec(memory_space=pltpu.VMEM)
    return pl.pallas_call(
        functools.partial(kernel, bricks, sects, slabs),
        out_shape=jax.ShapeDtypeStruct((dense_last.shape[1], peers * cap), jnp.float32),
        in_specs=[anywhere, anywhere, local, local, local, anywhere, anywhere, local],
        out_specs=local,
        scratch_shapes=[
            pltpu.VMEM(geometry.shape, jnp.bfloat16),
            pltpu.VMEM((channels * span_y, span_z), jnp.float32),
            pltpu.VMEM(padded, jnp.bfloat16),
            pltpu.VMEM(padded, jnp.bfloat16),
            pltpu.VMEM(conv_kernels.shape, jnp.bfloat16),
            pltpu.VMEM((3, 3 * channels, 3 * channels), jnp.bfloat16),
            pltpu.VMEM(dense_first.shape, jnp.bfloat16),
            pltpu.VMEM(dense_middle.shape, jnp.bfloat16),
            pltpu.VMEM((2, 8, width), jnp.float32),
            pltpu.VMEM((peers, 8, width), jnp.float32),
            pltpu.SemaphoreType.DMA((4,)),
            pltpu.SemaphoreType.DMA((2, 8)),
            pltpu.SemaphoreType.DMA((2, 8)),
            pltpu.SemaphoreType.DMA((peers,)),
            pltpu.SemaphoreType.DMA((peers,)),
        ],
        compiler_params=pltpu.CompilerParams(
            collective_id=0, has_side_effects=True, vmem_limit_bytes=48 * 2**20
        ),
    )(
        geometry,
        conv_kernels,
        point_place,
        point_attr.T,
        destination.reshape(1, count),
        dense_first,
        dense_middle,
        dense_last,
    )


def solution(mesh):
    sizes = tuple(mesh.shape[axis] for axis in ("brick", "sect", "slab"))
    in_specs = (
        P(None, ("case", "brick"), ("sect", "slab"), None),
        P(),
        P(None, ("case", "brick", "sect", "slab")),
        P(("case", "brick", "sect", "slab"), None),
        P(("case", "brick", "sect", "slab"), None),
        P(),
        P(),
        P(),
    )
    out_specs = P(None, ("case", "brick", "sect", "slab"))
    return jax.shard_map(
        functools.partial(on_device, sizes),
        mesh=mesh,
        in_specs=in_specs,
        out_specs=out_specs,
        check_vma=False,
    )
```

time: 86.6 us -> 32.8 us (0.38)
  Pallas kernels: 0 us -> 24 us
  starting transfers between devices: 19.7 us -> 0 us
  matrix products: 14.8 us -> 0 us
  blocking collectives: 14.6 us -> 0 us
  local copies, waits for them, and re-layouts: 20.8 us -> 8.31 us
  waiting for transfers between devices: 10.4 us -> 0 us
  other arithmetic: 5.07 us -> 0 us
    pallas_call x0 -> x1, Pallas kernels: none -> 24 us  [on_device(): pl.pallas_call(functools.partial(kernel, bricks, sects, slabs), out_shape...]
    ppermute x8 -> x0, starting transfers between devices: 19.7 us -> none  [the longest x4 14.4 us: extended(): before = lax.ppermute(last, axis, up)]
    all_to_all x1 -> x0, blocking collectives: 14.6 us -> none  [on_device(): lax.all_to_all(outbox, ('brick', 'sect'), split_axis=1, concat_axis=1, ti...]
    ppermute x8 -> x0, waiting for transfers between devices: 10.4 us -> none  [the longest x4 7.42 us: extended(): after = lax.ppermute(leading, axis, down)]
    dot_general x7 -> x0, matrix products: 10.3 us -> none  [the longest x4 6.27 us: network(): jnp.dot(activity, middle_weights[ordinal], preferred_element_type=jnp.flo...]
    conv_general_dilated x1 -> x0, matrix products: 4.51 us -> none  [convolve(): lax.conv_general_dilated(features_now[None], kernel, (1, 1, 1), ((0, 0),...]
    conv_general_dilated x4 -> x0, local copies, waits for them, and re-layouts: 4.4 us -> none  [convolve(): lax.conv_general_dilated(features_now[None], kernel, (1, 1, 1), ((0, 0),...]
    unnamed x25 -> x17, local copies, waits for them, and re-layouts: 5.7 us -> 8.31 us
  transfers between devices with their start and end apart: 8 -> 0, of which waited for: 5 -> 0; matrix products, arithmetic and copies ran while one was open for 10% -> 0% of each run, Pallas kernels for 0% -> 0%
where the time goes in v1:
time: 32.8 us; the launch traced here: 32.3 us
  Pallas kernels  24 us (73%)
  local copies, waits for them, and re-layouts  8.31 us (25%)
    pallas_call x1, Pallas kernels, on_device(): pl.pallas_call(functools.partial(kernel, bricks, sects, slabs), out_shape...  24 us
    unnamed x17, local copies, waits for them, and re-layouts  8.31 us

profile of v1, /device:TPU:0, one launch (start us, length us, event | category | flops | bytes accessed | tf_op | source)
XLA Modules:
  0.0 32.3 jit_solution(12420162167649860621)
XLA Ops:
  0.0 0.0 copy-start
  0.0 1.9 %copy-done = bf16[2,3,512,512]{3,2,1,0:T(8,128)(2,1)S(1)} copy-done((bf16[2,3,512,512]{3,2,1,0:T(8,128)(2,1)S(1)}, bf16[2,3,512,512]{3,2,1,0:T(8,128)(2,1)}, u32[]{:S(2)}) %copy-start) | copy-done | bytes 3145752
  1.9 0.0 copy-start.1
  1.9 1.0 %copy-done.1 = bf16[64,4,8,128]{3,2,1,0:T(8,128)(2,1)S(1)} copy-done((bf16[64,4,8,128]{3,2,1,0:T(8,128)(2,1)S(1)}, bf16[64,4,8,128]{3,2,1,0:T(8,128)(2,1)}, u32[]{:S(2)}) %copy-start.1) | copy-done | bytes 524312
  2.9 0.0 copy-start.2
  2.9 1.0 %copy-done.2 = bf16[1,3,3,3,64,64]{5,4,3,2,1,0:T(8,128)(2,1)S(1)} copy-done((bf16[1,3,3,3,64,64]{5,4,3,2,1,0:T(8,128)(2,1)S(1)}, bf16[1,3,3,3,64,64]{5,4,3,2,1,0:T(8,128)(2,1)}, u32[]{:S(2)}) %copy-start.2) | copy-done | bytes 221208
  3.9 0.0 copy-start.3
  3.9 0.9 %copy-done.3 = bf16[2,128,512]{2,1,0:T(8,128)(2,1)S(1)} copy-done((bf16[2,128,512]{2,1,0:T(8,128)(2,1)S(1)}, bf16[2,128,512]{2,1,0:T(8,128)(2,1)}, u32[]{:S(2)}) %copy-start.3) | copy-done | bytes 262168
  4.9 0.0 copy-start.4
  4.9 0.8 %copy-done.4 = bf16[256,64]{0,1:T(8,128)(2,1)S(1)} copy-done((bf16[256,64]{0,1:T(8,128)(2,1)S(1)}, bf16[256,64]{0,1:T(8,128)(2,1)}, u32[]{:S(2)}) %copy-start.4) | copy-done | bytes 32792
  5.7 0.0 copy-start.5
  5.7 0.7 %copy-done.5 = bf16[2,4,512]{2,1,0:T(4,128)(2,1)S(1)} copy-done((bf16[2,4,512]{2,1,0:T(4,128)(2,1)S(1)}, bf16[2,4,512]{2,1,0:T(4,128)(2,1)}, u32[]{:S(2)}) %copy-start.5) | copy-done | bytes 8216
  6.4 0.0 copy-start.6
  6.4 0.7 %copy-done.6 = f32[3,256]{1,0:T(4,128)S(1)} copy-done((f32[3,256]{1,0:T(4,128)S(1)}, f32[3,256]{1,0:T(4,128)}, u32[]{:S(2)}) %copy-start.6) | copy-done | bytes 3096
  7.0 0.0 copy-start.7
  7.0 0.7 %copy-done.7 = s32[256,1]{0,1:T(1,128)S(1)} copy-done((s32[256,1]{0,1:T(1,128)S(1)}, s32[256,1]{0,1:T(1,128)}, u32[]{:S(2)}) %copy-start.7) | copy-done | bytes 1048
  7.7 24.0 %shard_map.82 = f32[4,320]{1,0:T(4,128)S(1)} custom-call(bf16[64,4,8,128]{3,2,1,0:T(8,128)(2,1)S(1)} %copy-done.1, bf16[1,3,3,3,64,64]{5,4,3,2,1,0:T(8,128)(2,1)S(1)} %copy-done.2, f32[3,256]{1,0:T(4,128)S(1)} %copy-done.6, bf16[64,256]{1,0:T(8,128)(2,1)S(1)} %bitcast.2, s32[1,256]{1,0:T(1,128)S(1)} %bitcast.3, bf16[2,128,512]{2,1,0:T(8,128)(2,1)S(1)} %copy-done.3, ...), custom_call_target="tpu_custom_call" | custom-call | tf_op jit(solution)/shard_map/pallas_call | solution.py:294
  31.7 0.6 %copy.10 = f32[4,320]{1,0:T(4,128)} copy(f32[4,320]{1,0:T(4,128)S(1)} %shard_map.82) | data formatting | bytes 10240
Async XLA Ops:
  0.0 1.9 %copy-start = (bf16[2,3,512,512]{3,2,1,0:T(8,128)(2,1)S(1)}, bf16[2,3,512,512]{3,2,1,0:T(8,128)(2,1)}, u32[]{:S(2)}) copy-start(bf16[2,3,512,512]{3,2,1,0:T(8,128)(2,1)} %middle.1) | copy-start | bytes 9437188
  1.9 1.0 %copy-start.1 = (bf16[64,4,8,128]{3,2,1,0:T(8,128)(2,1)S(1)}, bf16[64,4,8,128]{3,2,1,0:T(8,128)(2,1)}, u32[]{:S(2)}) copy-start(bf16[64,4,8,128]{3,2,1,0:T(8,128)(2,1)} %geometry.1) | copy-start | bytes 1572868
  2.9 1.0 %copy-start.2 = (bf16[1,3,3,3,64,64]{5,4,3,2,1,0:T(8,128)(2,1)S(1)}, bf16[1,3,3,3,64,64]{5,4,3,2,1,0:T(8,128)(2,1)}, u32[]{:S(2)}) copy-start(bf16[1,3,3,3,64,64]{5,4,3,2,1,0:T(8,128)(2,1)} %kernels.1) | copy-start | bytes 663556
  3.9 0.9 %copy-start.3 = (bf16[2,128,512]{2,1,0:T(8,128)(2,1)S(1)}, bf16[2,128,512]{2,1,0:T(8,128)(2,1)}, u32[]{:S(2)}) copy-start(bf16[2,128,512]{2,1,0:T(8,128)(2,1)} %first.1) | copy-start | bytes 786436
  4.9 0.8 %copy-start.4 = (bf16[256,64]{0,1:T(8,128)(2,1)S(1)}, bf16[256,64]{0,1:T(8,128)(2,1)}, u32[]{:S(2)}) copy-start(bf16[256,64]{0,1:T(8,128)(2,1)} %param.11) | copy-start | bytes 98308
  5.7 0.7 %copy-start.5 = (bf16[2,4,512]{2,1,0:T(4,128)(2,1)S(1)}, bf16[2,4,512]{2,1,0:T(4,128)(2,1)}, u32[]{:S(2)}) copy-start(bf16[2,4,512]{2,1,0:T(4,128)(2,1)} %last.1) | copy-start | bytes 24580
  6.4 0.7 %copy-start.6 = (f32[3,256]{1,0:T(4,128)S(1)}, f32[3,256]{1,0:T(4,128)}, u32[]{:S(2)}) copy-start(f32[3,256]{1,0:T(4,128)} %place.1) | copy-start | bytes 9220
  7.0 0.7 %copy-start.7 = (s32[256,1]{0,1:T(1,128)S(1)}, s32[256,1]{0,1:T(1,128)}, u32[]{:S(2)}) copy-start(s32[256,1]{0,1:T(1,128)} %param.12) | copy-start | bytes 3076

commit v2 on v1

v2 whole, which is shorter than its diff:
```python
import functools
import math

import jax
import jax.numpy as jnp
from jax import lax
from jax.experimental import pallas as pl
from jax.experimental.pallas import tpu as pltpu
from jax.sharding import PartitionSpec as P

MESH = pl.DeviceIdType.MESH
DIRECTIONS = ((1, 0), (-1, 0), (1, 1), (1, -1), (-1, 1), (-1, -1), (0, 1), (0, -1))
NT = (((1,), (1,)), ((), ()))


def hat(offset):
    return jnp.maximum(0.0, 1.0 - jnp.abs(offset))


def gelu(value):
    scale = (2.0 / math.pi) ** 0.5
    middle = 0.5 * value
    return middle + middle * jnp.tanh(value * (scale + (scale * 0.044715) * (value * value)))


def dot(a, b):
    return jnp.dot(a, b, preferred_element_type=jnp.float32)


def send_range(step, size):
    return {1: pl.ds(size, 1), -1: pl.ds(1, 1), 0: pl.ds(1, size)}[step]


def land_range(step, size):
    return {1: pl.ds(0, 1), -1: pl.ds(size + 1, 1), 0: pl.ds(1, size)}[step]


def kernel(
    bricks,
    sects,
    slabs,
    geometry,
    kernels,
    place_in,
    attr_in,
    target_in,
    first,
    middle,
    last_in,
    out,
    geo,
    wide,
    pad,
    lat,
    taps,
    taps_t,
    place,
    attr,
    target,
    first_v,
    middle_v,
    last,
    near_place,
    partial,
    incoming,
    outbox,
    inbox,
    local_sem,
    send_sem,
    recv_sem,
    value_send,
    value_recv,
):
    channels, span_x, span_y, span_z = geo.shape
    count = place.shape[1]
    peers = bricks * sects
    cap = 5 * count // (4 * peers)
    half = peers // 2 * cap
    brick = lax.axis_index("brick")
    sect = lax.axis_index("sect")
    slab = lax.axis_index("slab")
    column = sect * slabs + slab
    columns = sects * slabs
    me = brick * sects + sect
    linear = me * slabs + slab
    everyone = peers * slabs

    loads = [
        pltpu.make_async_copy(source, landing, local_sem.at[i])
        for i, (source, landing) in enumerate(
            (
                (geometry, geo),
                (place_in, place),
                (kernels, taps),
                (target_in, target),
                (attr_in, attr),
                (first, first_v),
                (middle, middle_v),
                (last_in, last),
            )
        )
    ]
    for load in loads:
        load.start()

    barrier = pltpu.get_barrier_semaphore()
    for j in range(1, everyone):
        other = lax.rem(linear + j, everyone)
        pl.semaphore_signal(
            barrier,
            inc=1,
            device_id={
                "brick": other // columns,
                "sect": other % columns // slabs,
                "slab": other % slabs,
            },
            device_id_type=MESH,
        )

    def inside(dx, dy):
        b, c = brick + dx, column + dy
        return (b >= 0) & (b < bricks) & (c >= 0) & (c < columns)

    def remote(source, landing, phase, k):
        dx, dy = DIRECTIONS[k]
        c = column + dy
        return pltpu.make_async_remote_copy(
            src_ref=source,
            dst_ref=landing,
            send_sem=send_sem.at[phase, k],
            recv_sem=recv_sem.at[phase, k],
            device_id={"brick": brick + dx, "sect": c // slabs, "slab": c % slabs},
            device_id_type=MESH,
        )

    def halo_copy(phase, k):
        dx, dy = DIRECTIONS[k]
        if phase == 1 and dy == 0:
            return remote(partial.at[k], incoming.at[k], phase, k)
        if phase == 2:
            return remote(place, near_place.at[k], phase, k)
        buffer = (pad, lat)[phase]
        return remote(
            buffer.at[send_range(dx, span_x), send_range(dy, span_y)],
            buffer.at[land_range(dx, span_x), land_range(dy, span_y)],
            phase,
            k,
        )

    def start(phase, which):
        for k in which:
            @pl.when(inside(*DIRECTIONS[k]))
            def _():
                halo_copy(phase, k).start()

    def land(phase, which):
        for k in which:
            dx, dy = DIRECTIONS[k]

            @pl.when(inside(-dx, -dy))
            def _():
                halo_copy(phase, k).wait_recv()

    def drain(phase, which):
        for k in which:
            @pl.when(inside(*DIRECTIONS[k]))
            def _():
                halo_copy(phase, k).wait_send()

    def turn(x):
        base = x * channels * span_y
        wide[base:base + channels * span_y] = (
            geo[:, x].astype(jnp.float32).reshape(channels * span_y, span_z)
        )
        for y in range(span_y):
            pad[x + 1, y + 1] = wide[pl.ds(base + y, channels, stride=span_y), :].astype(
                jnp.bfloat16
            )

    loads[0].wait()
    turn(0)
    turn(span_x - 1)
    loads[1].wait()
    pl.semaphore_wait(barrier, everyone - 1)
    start(0, range(6))
    start(2, (0, 1))
    for x in range(1, span_x - 1):
        turn(x)
    start(0, (6, 7))

    for k, (dx, dy) in enumerate(DIRECTIONS):
        @pl.when(jnp.logical_not(inside(-dx, -dy)))
        def _():
            for buffer in (pad, lat):
                region = buffer.at[land_range(dx, span_x), land_range(dy, span_y)]
                region[...] = jnp.zeros(region.shape, jnp.bfloat16)
            if dy == 0:
                near_place[k] = jnp.zeros(near_place.shape[1:], jnp.float32)
                incoming[k] = jnp.zeros(incoming.shape[1:], jnp.bfloat16)

    loads[2].wait()
    for a in range(3):
        for b in range(3):
            for e in range(3):
                tap = taps[0, a, b, e].astype(jnp.float32).T.astype(jnp.bfloat16)
                low = (a * 3 + b) * channels
                taps_t[e * channels:(e + 1) * channels, low:low + channels] = tap

    cells = lax.broadcasted_iota(jnp.int32, (span_z, count), 0).astype(jnp.float32) + 0.5

    def weights(points):
        local_x = points[0:1, :] * span_x
        local_y = points[1:2, :] * span_y
        local_z = points[2:3, :] * span_z
        return (
            [hat(local_x - (x - 0.5)) for x in range(span_x + 2)],
            [hat(local_y - (y - 0.5)) for y in range(span_y + 2)],
            hat(local_z - cells).astype(jnp.bfloat16),
        )

    own_weights = weights(place)

    loads[3].wait()
    named = lax.broadcasted_iota(jnp.int32, (peers, count), 0)
    onehot = named == target[...]
    earlier = lax.broadcasted_iota(jnp.int32, (count, count), 0) < lax.broadcasted_iota(
        jnp.int32, (count, count), 1
    )
    before = dot(onehot.astype(jnp.bfloat16), earlier.astype(jnp.bfloat16))
    named_brick = lax.div(named, jnp.int32(sects))
    named_sect = named - named_brick * sects
    upper = (named_sect >= sects // 2).astype(jnp.int32)
    block = upper * (peers // 2) + named_brick * (sects // 2) + named_sect - upper * (sects // 2)
    position = jnp.sum(
        jnp.where(onehot, before + (block * cap).astype(jnp.float32), 0.0), axis=0, keepdims=True
    )
    slots = lax.broadcasted_iota(jnp.int32, (2 * half, count), 0)
    gather = (slots == position.astype(jnp.int32)).astype(jnp.bfloat16)

    lane = lax.broadcasted_iota(jnp.int32, (channels, span_z), 1)

    def product(x, y, low, high):
        near = jnp.concatenate(
            [
                jnp.concatenate(
                    [pad[x + a, y + i:y + i + 3].reshape(3 * channels, span_z) for i in (0, 1)],
                    axis=1,
                )
                for a in range(low, high)
            ],
            axis=0,
        )
        return dot(taps_t[:, low * 3 * channels:high * 3 * channels], near)

    def finish(x, y, pair):
        for i in (0, 1):
            part = pair[:, i * span_z:(i + 1) * span_z]
            left = pltpu.roll(part[:channels], 1, 1)
            right = pltpu.roll(part[2 * channels:], span_z - 1, 1)
            response = (
                part[channels:2 * channels]
                + jnp.where(lane == 0, 0.0, left)
                + jnp.where(lane == span_z - 1, 0.0, right)
            )
            old = pad[x + 1, y + i + 1].astype(jnp.float32)
            lat[x + 1, y + i + 1] = (old + gelu(response)).astype(jnp.bfloat16)

    land(0, (6, 7))
    for x in range(1, span_x - 1):
        for y in range(0, span_y, 2):
            finish(x, y, product(x, y, 0, 3))
    early = [
        [product(x, y, low, high) for y in range(0, span_y, 2)]
        for x, low, high in ((0, 1, 3), (span_x - 1, 0, 2))
    ]
    land(0, range(6))
    for side, (x, a) in enumerate(((0, 0), (span_x - 1, 2))):
        for y in range(0, span_y, 2):
            finish(x, y, early[side][y // 2] + product(x, y, a, a + 1))
    start(1, range(2, 8))

    def sample(of_weights, x, weight, low, high):
        weight_y, weight_z = of_weights[1:]
        part = dot(lat[x, low:high].reshape((high - low) * channels, span_z), weight_z)
        inner = None
        for y in range(low, high):
            term = part[(y - low) * channels:(y - low + 1) * channels] * weight_y[y]
            inner = term if inner is None else inner + term
        return inner * weight

    land(2, (0, 1))
    for k, x, weight in ((0, span_x, 0), (1, 1, span_x + 1)):
        theirs = weights(near_place.at[1 - k])
        partial[k] = sample(theirs, x, theirs[0][weight], 1, span_y + 1).astype(jnp.bfloat16)
    start(1, (0, 1))

    weight_x = own_weights[0]
    total = None
    for x in range(1, span_x + 1):
        term = sample(own_weights, x, weight_x[x], 1, span_y + 1)
        total = term if total is None else total + term
    land(1, range(2, 8))
    for x in range(span_x + 2):
        total = total + sample(own_weights, x, weight_x[x], 0, 1)
        total = total + sample(own_weights, x, weight_x[x], span_y + 1, span_y + 2)
    for load in loads[4:]:
        load.wait()
    land(1, (0, 1))
    total = total + incoming[0].astype(jnp.float32) + incoming[1].astype(jnp.float32)
    row = jnp.concatenate([total.astype(jnp.bfloat16), attr[...]], axis=0)
    table = lax.dot_general(gather, row, NT, preferred_element_type=jnp.float32)
    table = table.astype(jnp.bfloat16)

    acts = [
        gelu(dot(table[s * half:(s + 1) * half], first_v[s])).astype(jnp.bfloat16) for s in range(2)
    ]
    for layer in range(middle_v.shape[1]):
        acts = [gelu(dot(acts[s], middle_v[s, layer])).astype(jnp.bfloat16) for s in range(2)]
    outbox[...] = jnp.zeros(outbox.shape, jnp.float32)
    for s in range(2):
        value = lax.dot_general(last[s], acts[s], NT, preferred_element_type=jnp.float32)
        outbox[s, 0:value.shape[0], 0:half] = value

    def value_copy(j):
        other = lax.rem(me + j, peers)
        there = other % sects
        return pltpu.make_async_remote_copy(
            src_ref=outbox.at[there // (sects // 2)],
            dst_ref=inbox.at[me],
            send_sem=value_send.at[j],
            recv_sem=value_recv.at[j],
            device_id={"brick": other // sects, "sect": there},
            device_id_type=MESH,
        )

    for j in range(1, peers):
        value_copy(j).start()
    inbox[me] = outbox[sect // (sects // 2)]
    drain(0, range(8))
    drain(1, range(8))
    drain(2, (0, 1))
    for j in range(1, peers):
        value_copy(j).wait()

    width = inbox.shape[2]
    own = (brick * (sects // 2) + sect % (sects // 2)) * cap
    rolled = pltpu.roll(inbox[...].reshape(peers * 8, width), lax.rem(width - own, width), 1)
    for i in range(peers):
        out[:, i * cap:(i + 1) * cap] = rolled[i * 8:i * 8 + out.shape[0], 0:cap]


def on_device(
    sizes,
    geometry,
    conv_kernels,
    point_place,
    point_attr,
    destination,
    dense_first,
    dense_middle,
    dense_last,
):
    bricks, sects, slabs = sizes
    channels, span_x, span_y, span_z = geometry.shape
    count = point_place.shape[1]
    peers = bricks * sects
    cap = 5 * count // (4 * peers)
    width = -(-(peers // 2 * cap) // 128) * 128
    padded = (span_x + 2, span_y + 2, channels, span_z)
    attr = point_attr.T
    target = destination.reshape(1, count)
    return pl.pallas_call(
        functools.partial(kernel, bricks, sects, slabs),
        out_shape=jax.ShapeDtypeStruct((dense_last.shape[1], peers * cap), jnp.float32),
        in_specs=[pl.BlockSpec(memory_space=pl.ANY)] * 8,
        out_specs=pl.BlockSpec(memory_space=pltpu.VMEM),
        scratch_shapes=[
            pltpu.VMEM(geometry.shape, jnp.bfloat16),
            pltpu.VMEM((span_x * channels * span_y, span_z), jnp.float32),
            pltpu.VMEM(padded, jnp.bfloat16),
            pltpu.VMEM(padded, jnp.bfloat16),
            pltpu.VMEM(conv_kernels.shape, jnp.bfloat16),
            pltpu.VMEM((3 * channels, 9 * channels), jnp.bfloat16),
            pltpu.VMEM(point_place.shape, jnp.float32),
            pltpu.VMEM(attr.shape, jnp.bfloat16),
            pltpu.VMEM(target.shape, jnp.int32),
            pltpu.VMEM(dense_first.shape, jnp.bfloat16),
            pltpu.VMEM(dense_middle.shape, jnp.bfloat16),
            pltpu.VMEM(dense_last.shape, jnp.bfloat16),
            pltpu.VMEM((2,) + point_place.shape, jnp.float32),
            pltpu.VMEM((2, channels, count), jnp.bfloat16),
            pltpu.VMEM((2, channels, count), jnp.bfloat16),
            pltpu.VMEM((2, 8, width), jnp.float32),
            pltpu.VMEM((peers, 8, width), jnp.float32),
            pltpu.SemaphoreType.DMA((8,)),
            pltpu.SemaphoreType.DMA((3, 8)),
            pltpu.SemaphoreType.DMA((3, 8)),
            pltpu.SemaphoreType.DMA((peers,)),
            pltpu.SemaphoreType.DMA((peers,)),
        ],
        compiler_params=pltpu.CompilerParams(
            collective_id=0, has_side_effects=True, vmem_limit_bytes=60 * 2**20
        ),
    )(
        geometry,
        conv_kernels,
        point_place,
        attr,
        target,
        dense_first,
        dense_middle,
        dense_last,
    )


def solution(mesh):
    sizes = tuple(mesh.shape[axis] for axis in ("brick", "sect", "slab"))
    in_specs = (
        P(None, ("case", "brick"), ("sect", "slab"), None),
        P(),
        P(None, ("case", "brick", "sect", "slab")),
        P(("case", "brick", "sect", "slab"), None),
        P(("case", "brick", "sect", "slab"), None),
        P(),
        P(),
        P(),
    )
    out_specs = P(None, ("case", "brick", "sect", "slab"))
    return jax.shard_map(
        functools.partial(on_device, sizes),
        mesh=mesh,
        in_specs=in_specs,
        out_specs=out_specs,
        check_vma=False,
    )
```

time: 32.8 us -> 23.2 us (0.71)
  local copies, waits for them, and re-layouts: 8.31 us -> 1.29 us
  Pallas kernels: 24 us -> 21.7 us
    unnamed x17 -> x1, local copies, waits for them, and re-layouts: 8.31 us -> 1.29 us
    pallas_call x1, Pallas kernels: 24 us -> 21.7 us  [on_device(): pl.pallas_call(functools.partial(kernel, bricks, sects, slabs), out_shape...]
where the time goes in v2:
time: 23.2 us; the launch traced here: 23 us
  Pallas kernels  21.7 us (94%)
  local copies, waits for them, and re-layouts  1.29 us (6%)
    pallas_call x1, Pallas kernels, on_device(): pl.pallas_call(functools.partial(kernel, bricks, sects, slabs), out_shape...  21.7 us
    unnamed x1, local copies, waits for them, and re-layouts  1.29 us

profile of v2, /device:TPU:0, one launch (start us, length us, event | category | flops | bytes accessed | tf_op | source)
XLA Modules:
  0.0 23.0 jit_solution(4235449126802655121)
XLA Ops:
  0.0 21.7 %shard_map.82 = f32[4,320]{1,0:T(4,128)} custom-call(bf16[64,4,8,128]{3,2,1,0:T(8,128)(2,1)} %geometry.1, bf16[1,3,3,3,64,64]{5,4,3,2,1,0:T(8,128)(2,1)} %kernels.1, f32[3,256]{1,0:T(4,128)} %place_in.1, bf16[64,256]{1,0:T(8,128)(2,1)} %bitcast.2, s32[1,256]{1,0:T(1,128)} %bitcast.3, bf16[2,128,512]{2,1,0:T(8,128)(2,1)} %first.1, ...), custom_call_target="tpu_custom_call" | custom-call | tf_op jit(solution)/shard_map/pallas_call | solution.py:372
  21.7 1.3 %copy.10 = f32[4,320]{1,0:T(4,128)} copy(f32[4,320]{1,0:T(4,128)} %shard_map.82) | data formatting | bytes 10240

commit v3 on v2

--- a/solution.py
+++ b/solution.py
@@ -63,6 +63,7 @@
     near_place,
     partial,
     incoming,
+    edge,
     outbox,
     inbox,
     local_sem,
@@ -85,14 +86,20 @@
     linear = me * slabs + slab
     everyone = peers * slabs
 
+    row_order = (0, span_x - 1) + tuple(range(1, span_x - 1))
+    row_loads = {
+        x: pltpu.make_async_copy(
+            geometry.at[:, pl.ds(x, 1)], geo.at[:, pl.ds(x, 1)], local_sem.at[8 + x]
+        )
+        for x in row_order
+    }
     loads = [
         pltpu.make_async_copy(source, landing, local_sem.at[i])
         for i, (source, landing) in enumerate(
             (
-                (geometry, geo),
                 (place_in, place),
+                (target_in, target),
                 (kernels, taps),
-                (target_in, target),
                 (attr_in, attr),
                 (first, first_v),
                 (middle, middle_v),
@@ -100,8 +107,6 @@
             )
         )
     ]
-    for load in loads:
-        load.start()
 
     barrier = pltpu.get_barrier_semaphore()
     for j in range(1, everyone):
@@ -117,6 +122,11 @@
             device_id_type=MESH,
         )
 
+    for x in row_order:
+        row_loads[x].start()
+    for load in loads:
+        load.start()
+
     def inside(dx, dy):
         b, c = brick + dx, column + dy
         return (b >= 0) & (b < bricks) & (c >= 0) & (c < columns)
@@ -137,6 +147,9 @@
         dx, dy = DIRECTIONS[k]
         if phase == 1 and dy == 0:
             return remote(partial.at[k], incoming.at[k], phase, k)
+        if phase == 0 and dy == 0:
+            row = pl.ds(span_x - 1 if dx == 1 else 0, 1)
+            return remote(geometry.at[:, row], edge.at[k], phase, k)
         if phase == 2:
             return remote(place, near_place.at[k], phase, k)
         buffer = (pad, lat)[phase]
@@ -167,44 +180,13 @@
             def _():
                 halo_copy(phase, k).wait_send()
 
-    def turn(x):
+    def turn(x, source):
         base = x * channels * span_y
-        wide[base:base + channels * span_y] = (
-            geo[:, x].astype(jnp.float32).reshape(channels * span_y, span_z)
+        wide[base:base + channels * span_y] = source.astype(jnp.float32).reshape(
+            channels * span_y, span_z
         )
         for y in range(span_y):
-            pad[x + 1, y + 1] = wide[pl.ds(base + y, channels, stride=span_y), :].astype(
-                jnp.bfloat16
-            )
-
-    loads[0].wait()
-    turn(0)
-    turn(span_x - 1)
-    loads[1].wait()
-    pl.semaphore_wait(barrier, everyone - 1)
-    start(0, range(6))
-    start(2, (0, 1))
-    for x in range(1, span_x - 1):
-        turn(x)
-    start(0, (6, 7))
-
-    for k, (dx, dy) in enumerate(DIRECTIONS):
-        @pl.when(jnp.logical_not(inside(-dx, -dy)))
-        def _():
-            for buffer in (pad, lat):
-                region = buffer.at[land_range(dx, span_x), land_range(dy, span_y)]
-                region[...] = jnp.zeros(region.shape, jnp.bfloat16)
-            if dy == 0:
-                near_place[k] = jnp.zeros(near_place.shape[1:], jnp.float32)
-                incoming[k] = jnp.zeros(incoming.shape[1:], jnp.bfloat16)
-
-    loads[2].wait()
-    for a in range(3):
-        for b in range(3):
-            for e in range(3):
-                tap = taps[0, a, b, e].astype(jnp.float32).T.astype(jnp.bfloat16)
-                low = (a * 3 + b) * channels
-                taps_t[e * channels:(e + 1) * channels, low:low + channels] = tap
+            pad[x, y + 1] = wide[pl.ds(base + y, channels, stride=span_y), :].astype(jnp.bfloat16)
 
     cells = lax.broadcasted_iota(jnp.int32, (span_z, count), 0).astype(jnp.float32) + 0.5
 
@@ -218,9 +200,22 @@
             hat(local_z - cells).astype(jnp.bfloat16),
         )
 
+    pl.semaphore_wait(barrier, everyone - 1)
+    start(0, (0, 1))
+    loads[0].wait()
+    start(2, (0, 1))
+    for x in row_order[:2]:
+        row_loads[x].wait()
+        turn(x + 1, geo[:, x])
+    start(0, range(2, 6))
+    for x in row_order[2:]:
+        row_loads[x].wait()
+        turn(x + 1, geo[:, x])
+    start(0, (6, 7))
+
     own_weights = weights(place)
 
-    loads[3].wait()
+    loads[1].wait()
     named = lax.broadcasted_iota(jnp.int32, (peers, count), 0)
     onehot = named == target[...]
     earlier = lax.broadcasted_iota(jnp.int32, (count, count), 0) < lax.broadcasted_iota(
@@ -237,6 +232,26 @@
     slots = lax.broadcasted_iota(jnp.int32, (2 * half, count), 0)
     gather = (slots == position.astype(jnp.int32)).astype(jnp.bfloat16)
 
+    for k, (dx, dy) in enumerate(DIRECTIONS):
+        @pl.when(jnp.logical_not(inside(-dx, -dy)))
+        def _():
+            if dy != 0:
+                for buffer in (pad, lat):
+                    region = buffer.at[land_range(dx, span_x), land_range(dy, span_y)]
+                    region[...] = jnp.zeros(region.shape, jnp.bfloat16)
+            else:
+                edge[k] = jnp.zeros(edge.shape[1:], jnp.bfloat16)
+                near_place[k] = jnp.zeros(near_place.shape[1:], jnp.float32)
+                incoming[k] = jnp.zeros(incoming.shape[1:], jnp.bfloat16)
+
+    loads[2].wait()
+    for a in range(3):
+        for b in range(3):
+            for e in range(3):
+                tap = taps[0, a, b, e].astype(jnp.float32).T.astype(jnp.bfloat16)
+                low = (a * 3 + b) * channels
+                taps_t[e * channels:(e + 1) * channels, low:low + channels] = tap
+
     lane = lax.broadcasted_iota(jnp.int32, (channels, span_z), 1)
 
     def product(x, y, low, high):
@@ -274,6 +289,8 @@
         for x, low, high in ((0, 1, 3), (span_x - 1, 0, 2))
     ]
     land(0, range(6))
+    turn(0, edge[0, :, 0])
+    turn(span_x + 1, edge[1, :, 0])
     for side, (x, a) in enumerate(((0, 0), (span_x - 1, 2))):
         for y in range(0, span_y, 2):
             finish(x, y, early[side][y // 2] + product(x, y, a, a + 1))
@@ -303,7 +320,7 @@
     for x in range(span_x + 2):
         total = total + sample(own_weights, x, weight_x[x], 0, 1)
         total = total + sample(own_weights, x, weight_x[x], span_y + 1, span_y + 2)
-    for load in loads[4:]:
+    for load in loads[3:]:
         load.wait()
     land(1, (0, 1))
     total = total + incoming[0].astype(jnp.float32) + incoming[1].astype(jnp.float32)
@@ -371,12 +388,12 @@
     target = destination.reshape(1, count)
     return pl.pallas_call(
         functools.partial(kernel, bricks, sects, slabs),
-        out_shape=jax.ShapeDtypeStruct((dense_last.shape[1], peers * cap), jnp.float32),
+        out_shape=pltpu.VMEM((dense_last.shape[1], peers * cap), jnp.float32),
         in_specs=[pl.BlockSpec(memory_space=pl.ANY)] * 8,
         out_specs=pl.BlockSpec(memory_space=pltpu.VMEM),
         scratch_shapes=[
             pltpu.VMEM(geometry.shape, jnp.bfloat16),
-            pltpu.VMEM((span_x * channels * span_y, span_z), jnp.float32),
+            pltpu.VMEM(((span_x + 2) * channels * span_y, span_z), jnp.float32),
             pltpu.VMEM(padded, jnp.bfloat16),
             pltpu.VMEM(padded, jnp.bfloat16),
             pltpu.VMEM(conv_kernels.shape, jnp.bfloat16),
@@ -390,9 +407,10 @@
             pltpu.VMEM((2,) + point_place.shape, jnp.float32),
             pltpu.VMEM((2, channels, count), jnp.bfloat16),
             pltpu.VMEM((2, channels, count), jnp.bfloat16),
+            pltpu.VMEM((2, channels, 1, span_y, span_z), jnp.bfloat16),
             pltpu.VMEM((2, 8, width), jnp.float32),
             pltpu.VMEM((peers, 8, width), jnp.float32),
-            pltpu.SemaphoreType.DMA((8,)),
+            pltpu.SemaphoreType.DMA((8 + span_x,)),
             pltpu.SemaphoreType.DMA((3, 8)),
             pltpu.SemaphoreType.DMA((3, 8)),
             pltpu.SemaphoreType.DMA((peers,)),

time: 23.2 us -> 22.4 us (0.966)
  local copies, waits for them, and re-layouts: 1.29 us -> 0.6 us
    unnamed x1, local copies, waits for them, and re-layouts: 1.29 us -> 0.6 us
where the time goes in v3:
time: 22.4 us; the launch traced here: 22.3 us
  Pallas kernels  21.7 us (97%)
  local copies, waits for them, and re-layouts  0.6 us (3%)
    pallas_call x1, Pallas kernels, on_device(): pl.pallas_call(functools.partial(kernel, bricks, sects, slabs), out_shape...  21.7 us
    unnamed x1, local copies, waits for them, and re-layouts  0.6 us

profile of v3, /device:TPU:0, one launch (start us, length us, event | category | flops | bytes accessed | tf_op | source)
XLA Modules:
  0.0 22.3 jit_solution(10285054933987415198)
XLA Ops:
  0.0 21.7 %shard_map.82 = f32[4,320]{1,0:T(4,128)S(1)} custom-call(bf16[64,4,8,128]{3,2,1,0:T(8,128)(2,1)} %geometry.1, bf16[1,3,3,3,64,64]{5,4,3,2,1,0:T(8,128)(2,1)} %kernels.1, f32[3,256]{1,0:T(4,128)} %place_in.1, bf16[64,256]{1,0:T(8,128)(2,1)} %bitcast.2, s32[1,256]{1,0:T(1,128)} %bitcast.3, bf16[2,128,512]{2,1,0:T(8,128)(2,1)} %first.1, ...), custom_call_target="tpu_custom_call" | custom-call | tf_op jit(solution)/shard_map/pallas_call | solution.py:389
  21.7 0.6 %copy.10 = f32[4,320]{1,0:T(4,128)} copy(f32[4,320]{1,0:T(4,128)S(1)} %shard_map.82) | data formatting | bytes 10240

commit v4 on v3

--- a/solution.py
+++ b/solution.py
@@ -115,9 +115,9 @@
             barrier,
             inc=1,
             device_id={
-                "brick": other // columns,
-                "sect": other % columns // slabs,
-                "slab": other % slabs,
+                "brick": lax.div(other, columns),
+                "sect": lax.div(lax.rem(other, columns), slabs),
+                "slab": lax.rem(other, slabs),
             },
             device_id_type=MESH,
         )
@@ -139,7 +139,7 @@
             dst_ref=landing,
             send_sem=send_sem.at[phase, k],
             recv_sem=recv_sem.at[phase, k],
-            device_id={"brick": brick + dx, "sect": c // slabs, "slab": c % slabs},
+            device_id={"brick": brick + dx, "sect": lax.div(c, slabs), "slab": lax.rem(c, slabs)},
             device_id_type=MESH,
         )
 
@@ -212,6 +212,86 @@
         row_loads[x].wait()
         turn(x + 1, geo[:, x])
     start(0, (6, 7))
+
+    for k, (dx, dy) in enumerate(DIRECTIONS):
+        @pl.when(jnp.logical_not(inside(-dx, -dy)))
+        def _():
+            if dy != 0:
+                for buffer in (pad, lat):
+                    region = buffer.at[land_range(dx, span_x), land_range(dy, span_y)]
+                    region[...] = jnp.zeros(region.shape, jnp.bfloat16)
+            else:
+                edge[k] = jnp.zeros(edge.shape[1:], jnp.bfloat16)
+                near_place[k] = jnp.zeros(near_place.shape[1:], jnp.float32)
+                incoming[k] = jnp.zeros(incoming.shape[1:], jnp.bfloat16)
+
+    loads[2].wait()
+    for a in range(3):
+        for b in range(3):
+            for e in range(3):
+                tap = taps[0, a, b, e].astype(jnp.float32).T.astype(jnp.bfloat16)
+                low = (a * 3 + b) * channels
+                taps_t[e * channels:(e + 1) * channels, low:low + channels] = tap
+
+    lane = lax.broadcasted_iota(jnp.int32, (channels, span_z), 1)
+
+    def product(x, y, low, high):
+        near = jnp.concatenate(
+            [
+                jnp.concatenate(
+                    [pad[x + a, y + i:y + i + 3].reshape(3 * channels, span_z) for i in (0, 1)],
+                    axis=1,
+                )
+                for a in range(low, high)
+            ],
+            axis=0,
+        )
+        return dot(taps_t[:, low * 3 * channels:high * 3 * channels], near)
+
+    def finish(x, y, pair):
+        for i in (0, 1):
+            part = pair[:, i * span_z:(i + 1) * span_z]
+            left = pltpu.roll(part[:channels], 1, 1)
+            right = pltpu.roll(part[2 * channels:], span_z - 1, 1)
+            response = (
+                part[channels:2 * channels]
+                + jnp.where(lane == 0, 0.0, left)
+                + jnp.where(lane == span_z - 1, 0.0, right)
+            )
+            old = pad[x + 1, y + i + 1].astype(jnp.float32)
+            lat[x + 1, y + i + 1] = (old + gelu(response)).astype(jnp.bfloat16)
+
+    land(0, (6, 7))
+    for x in range(1, span_x - 1):
+        for y in range(0, span_y, 2):
+            finish(x, y, product(x, y, 0, 3))
+    early = [
+        [product(x, y, low, high) for y in range(0, span_y, 2)]
+        for x, low, high in ((0, 1, 3), (span_x - 1, 0, 2))
+    ]
+    land(2, (0, 1))
+    theirs = [weights(near_place.at[1 - k]) for k in (0, 1)]
+    land(0, range(6))
+    turn(0, edge[0, :, 0])
+    turn(span_x + 1, edge[1, :, 0])
+    for side, (x, a) in enumerate(((0, 0), (span_x - 1, 2))):
+        for y in range(0, span_y, 2):
+            finish(x, y, early[side][y // 2] + product(x, y, a, a + 1))
+    start(1, range(2, 8))
+
+    def sample(of_weights, x, weight, low, high):
+        weight_y, weight_z = of_weights[1:]
+        part = dot(lat[x, low:high].reshape((high - low) * channels, span_z), weight_z)
+        inner = None
+        for y in range(low, high):
+            term = part[(y - low) * channels:(y - low + 1) * channels] * weight_y[y]
+            inner = term if inner is None else inner + term
+        return inner * weight
+
+    for k, x, weight in ((0, span_x, 0), (1, 1, span_x + 1)):
+        weight_x = theirs[k][0][weight]
+        partial[k] = sample(theirs[k], x, weight_x, 1, span_y + 1).astype(jnp.bfloat16)
+        start(1, (k,))
 
     own_weights = weights(place)
 
@@ -232,94 +312,20 @@
     slots = lax.broadcasted_iota(jnp.int32, (2 * half, count), 0)
     gather = (slots == position.astype(jnp.int32)).astype(jnp.bfloat16)
 
-    for k, (dx, dy) in enumerate(DIRECTIONS):
-        @pl.when(jnp.logical_not(inside(-dx, -dy)))
-        def _():
-            if dy != 0:
-                for buffer in (pad, lat):
-                    region = buffer.at[land_range(dx, span_x), land_range(dy, span_y)]
-                    region[...] = jnp.zeros(region.shape, jnp.bfloat16)
-            else:
-                edge[k] = jnp.zeros(edge.shape[1:], jnp.bfloat16)
-                near_place[k] = jnp.zeros(near_place.shape[1:], jnp.float32)
-                incoming[k] = jnp.zeros(incoming.shape[1:], jnp.bfloat16)
-
-    loads[2].wait()
-    for a in range(3):
-        for b in range(3):
-            for e in range(3):
-                tap = taps[0, a, b, e].astype(jnp.float32).T.astype(jnp.bfloat16)
-                low = (a * 3 + b) * channels
-                taps_t[e * channels:(e + 1) * channels, low:low + channels] = tap
-
-    lane = lax.broadcasted_iota(jnp.int32, (channels, span_z), 1)
-
-    def product(x, y, low, high):
-        near = jnp.concatenate(
-            [
-                jnp.concatenate(
-                    [pad[x + a, y + i:y + i + 3].reshape(3 * channels, span_z) for i in (0, 1)],
-                    axis=1,
-                )
-                for a in range(low, high)
-            ],
-            axis=0,
-        )
-        return dot(taps_t[:, low * 3 * channels:high * 3 * channels], near)
-
-    def finish(x, y, pair):
-        for i in (0, 1):
-            part = pair[:, i * span_z:(i + 1) * span_z]
-            left = pltpu.roll(part[:channels], 1, 1)
-            right = pltpu.roll(part[2 * channels:], span_z - 1, 1)
-            response = (
-                part[channels:2 * channels]
-                + jnp.where(lane == 0, 0.0, left)
-                + jnp.where(lane == span_z - 1, 0.0, right)
-            )
-            old = pad[x + 1, y + i + 1].astype(jnp.float32)
-            lat[x + 1, y + i + 1] = (old + gelu(response)).astype(jnp.bfloat16)
-
-    land(0, (6, 7))
-    for x in range(1, span_x - 1):
-        for y in range(0, span_y, 2):
-            finish(x, y, product(x, y, 0, 3))
-    early = [
-        [product(x, y, low, high) for y in range(0, span_y, 2)]
-        for x, low, high in ((0, 1, 3), (span_x - 1, 0, 2))
-    ]
-    land(0, range(6))
-    turn(0, edge[0, :, 0])
-    turn(span_x + 1, edge[1, :, 0])
-    for side, (x, a) in enumerate(((0, 0), (span_x - 1, 2))):
-        for y in range(0, span_y, 2):
-            finish(x, y, early[side][y // 2] + product(x, y, a, a + 1))
-    start(1, range(2, 8))
-
-    def sample(of_weights, x, weight, low, high):
-        weight_y, weight_z = of_weights[1:]
-        part = dot(lat[x, low:high].reshape((high - low) * channels, span_z), weight_z)
-        inner = None
-        for y in range(low, high):
-            term = part[(y - low) * channels:(y - low + 1) * channels] * weight_y[y]
-            inner = term if inner is None else inner + term
-        return inner * weight
-
-    land(2, (0, 1))
-    for k, x, weight in ((0, span_x, 0), (1, 1, span_x + 1)):
-        theirs = weights(near_place.at[1 - k])
-        partial[k] = sample(theirs, x, theirs[0][weight], 1, span_y + 1).astype(jnp.bfloat16)
-    start(1, (0, 1))
-
-    weight_x = own_weights[0]
+
+    outbox[...] = jnp.zeros(outbox.shape, jnp.float32)
+    weight_x, weight_y, weight_z = own_weights
     total = None
     for x in range(1, span_x + 1):
         term = sample(own_weights, x, weight_x[x], 1, span_y + 1)
         total = term if total is None else total + term
     land(1, range(2, 8))
-    for x in range(span_x + 2):
-        total = total + sample(own_weights, x, weight_x[x], 0, 1)
-        total = total + sample(own_weights, x, weight_x[x], span_y + 1, span_y + 2)
+    for y in (0, span_y + 1):
+        part = dot(lat[:, y].reshape((span_x + 2) * channels, span_z), weight_z)
+        inner = part[:channels] * weight_x[0]
+        for x in range(1, span_x + 2):
+            inner = inner + part[x * channels:(x + 1) * channels] * weight_x[x]
+        total = total + inner * weight_y[y]
     for load in loads[3:]:
         load.wait()
     land(1, (0, 1))
@@ -333,26 +339,25 @@
     ]
     for layer in range(middle_v.shape[1]):
         acts = [gelu(dot(acts[s], middle_v[s, layer])).astype(jnp.bfloat16) for s in range(2)]
-    outbox[...] = jnp.zeros(outbox.shape, jnp.float32)
     for s in range(2):
         value = lax.dot_general(last[s], acts[s], NT, preferred_element_type=jnp.float32)
         outbox[s, 0:value.shape[0], 0:half] = value
 
     def value_copy(j):
         other = lax.rem(me + j, peers)
-        there = other % sects
+        there = lax.rem(other, sects)
         return pltpu.make_async_remote_copy(
-            src_ref=outbox.at[there // (sects // 2)],
+            src_ref=outbox.at[lax.div(there, sects // 2)],
             dst_ref=inbox.at[me],
             send_sem=value_send.at[j],
             recv_sem=value_recv.at[j],
-            device_id={"brick": other // sects, "sect": there},
+            device_id={"brick": lax.div(other, sects), "sect": there},
             device_id_type=MESH,
         )
 
     for j in range(1, peers):
         value_copy(j).start()
-    inbox[me] = outbox[sect // (sects // 2)]
+    inbox[me] = outbox[lax.div(sect, sects // 2)]
     drain(0, range(8))
     drain(1, range(8))
     drain(2, (0, 1))

time: 22.4 us -> 22.4 us (level)
  no operation moved by 1% of the time
where the time goes in v4:
time: 22.4 us; the launch traced here: 22.3 us
  Pallas kernels  21.7 us (97%)
  local copies, waits for them, and re-layouts  0.6 us (3%)
    pallas_call x1, Pallas kernels, on_device(): pl.pallas_call(functools.partial(kernel, bricks, sects, slabs), out_shape...  21.7 us
    unnamed x1, local copies, waits for them, and re-layouts  0.6 us

profile of v4, /device:TPU:0, one launch (start us, length us, event | category | flops | bytes accessed | tf_op | source)
XLA Modules:
  0.0 22.3 jit_solution(16405755373852382528)
XLA Ops:
  0.0 21.7 %shard_map.82 = f32[4,320]{1,0:T(4,128)S(1)} custom-call(bf16[64,4,8,128]{3,2,1,0:T(8,128)(2,1)} %geometry.1, bf16[1,3,3,3,64,64]{5,4,3,2,1,0:T(8,128)(2,1)} %kernels.1, f32[3,256]{1,0:T(4,128)} %place_in.1, bf16[64,256]{1,0:T(8,128)(2,1)} %bitcast.2, s32[1,256]{1,0:T(1,128)} %bitcast.3, bf16[2,128,512]{2,1,0:T(8,128)(2,1)} %first.1, ...), custom_call_target="tpu_custom_call" | custom-call | tf_op jit(solution)/shard_map/pallas_call | solution.py:394
  21.7 0.6 %copy.10 = f32[4,320]{1,0:T(4,128)} copy(f32[4,320]{1,0:T(4,128)S(1)} %shard_map.82) | data formatting | bytes 10240

commit v5 on v4

--- a/solution.py
+++ b/solution.py
@@ -108,28 +108,48 @@
         )
     ]
 
+    def inside(dx, dy):
+        b, c = brick + dx, column + dy
+        return (b >= 0) & (b < bricks) & (c >= 0) & (c < columns)
+
+    near_only = bricks <= 4 and columns <= 4
     barrier = pltpu.get_barrier_semaphore()
-    for j in range(1, everyone):
-        other = lax.rem(linear + j, everyone)
-        pl.semaphore_signal(
-            barrier,
-            inc=1,
-            device_id={
-                "brick": lax.div(other, columns),
-                "sect": lax.div(lax.rem(other, columns), slabs),
-                "slab": lax.rem(other, slabs),
-            },
-            device_id_type=MESH,
-        )
+    if near_only:
+        for dx, dy in DIRECTIONS:
+            @pl.when(inside(dx, dy))
+            def _():
+                pl.semaphore_signal(
+                    barrier,
+                    inc=1,
+                    device_id={
+                        "brick": brick + dx,
+                        "sect": lax.div(column + dy, slabs),
+                        "slab": lax.rem(column + dy, slabs),
+                    },
+                    device_id_type=MESH,
+                )
+        spread_x = 1 + (brick > 0).astype(jnp.int32) + (brick < bricks - 1).astype(jnp.int32)
+        spread_y = 1 + (column > 0).astype(jnp.int32) + (column < columns - 1).astype(jnp.int32)
+        expected = spread_x * spread_y - 1
+    else:
+        expected = everyone - 1
+        for j in range(1, everyone):
+            other = lax.rem(linear + j, everyone)
+            pl.semaphore_signal(
+                barrier,
+                inc=1,
+                device_id={
+                    "brick": lax.div(other, columns),
+                    "sect": lax.div(lax.rem(other, columns), slabs),
+                    "slab": lax.rem(other, slabs),
+                },
+                device_id_type=MESH,
+            )
 
     for x in row_order:
         row_loads[x].start()
     for load in loads:
         load.start()
-
-    def inside(dx, dy):
-        b, c = brick + dx, column + dy
-        return (b >= 0) & (b < bricks) & (c >= 0) & (c < columns)
 
     def remote(source, landing, phase, k):
         dx, dy = DIRECTIONS[k]
@@ -200,7 +220,7 @@
             hat(local_z - cells).astype(jnp.bfloat16),
         )
 
-    pl.semaphore_wait(barrier, everyone - 1)
+    pl.semaphore_wait(barrier, expected)
     start(0, (0, 1))
     loads[0].wait()
     start(2, (0, 1))
@@ -261,22 +281,27 @@
             old = pad[x + 1, y + i + 1].astype(jnp.float32)
             lat[x + 1, y + i + 1] = (old + gelu(response)).astype(jnp.bfloat16)
 
+    early = {}
+
+    def inner_rows(some):
+        for x in range(1, span_x - 1):
+            for y in some:
+                finish(x, y, product(x, y, 0, 3))
+        for x, low, high in ((0, 1, 3), (span_x - 1, 0, 2)):
+            for y in some:
+                early[x, y] = product(x, y, low, high)
+
+    inner_rows(range(2, span_y - 2, 2))
     land(0, (6, 7))
-    for x in range(1, span_x - 1):
-        for y in range(0, span_y, 2):
-            finish(x, y, product(x, y, 0, 3))
-    early = [
-        [product(x, y, low, high) for y in range(0, span_y, 2)]
-        for x, low, high in ((0, 1, 3), (span_x - 1, 0, 2))
-    ]
+    inner_rows((0, span_y - 2))
     land(2, (0, 1))
     theirs = [weights(near_place.at[1 - k]) for k in (0, 1)]
     land(0, range(6))
     turn(0, edge[0, :, 0])
     turn(span_x + 1, edge[1, :, 0])
-    for side, (x, a) in enumerate(((0, 0), (span_x - 1, 2))):
+    for x, a in ((0, 0), (span_x - 1, 2)):
         for y in range(0, span_y, 2):
-            finish(x, y, early[side][y // 2] + product(x, y, a, a + 1))
+            finish(x, y, early[x, y] + product(x, y, a, a + 1))
     start(1, range(2, 8))
 
     def sample(of_weights, x, weight, low, high):

time: 22.4 us -> 21.8 us (0.973)
  Pallas kernels: 21.7 us -> 21 us
    pallas_call x1, Pallas kernels: 21.7 us -> 21 us  [on_device(): pl.pallas_call(functools.partial(kernel, bricks, sects, slabs), out_shape...]
where the time goes in v5:
time: 21.8 us; the launch traced here: 21.6 us
  Pallas kernels  21 us (96%)
  local copies, waits for them, and re-layouts  0.6 us (3%)
    pallas_call x1, Pallas kernels, on_device(): pl.pallas_call(functools.partial(kernel, bricks, sects, slabs), out_shape...  21 us
    unnamed x1, local copies, waits for them, and re-layouts  0.6 us

profile of v5, /device:TPU:0, one launch (start us, length us, event | category | flops | bytes accessed | tf_op | source)
XLA Modules:
  0.0 21.6 jit_solution(9779140617532387552)
XLA Ops:
  0.0 21.0 %shard_map.82 = f32[4,320]{1,0:T(4,128)S(1)} custom-call(bf16[64,4,8,128]{3,2,1,0:T(8,128)(2,1)} %geometry.1, bf16[1,3,3,3,64,64]{5,4,3,2,1,0:T(8,128)(2,1)} %kernels.1, f32[3,256]{1,0:T(4,128)} %place_in.1, bf16[64,256]{1,0:T(8,128)(2,1)} %bitcast.2, s32[1,256]{1,0:T(1,128)} %bitcast.3, bf16[2,128,512]{2,1,0:T(8,128)(2,1)} %first.1, ...), custom_call_target="tpu_custom_call" | custom-call | tf_op jit(solution)/shard_map/pallas_call | solution.py:419
  21.0 0.6 %copy.10 = f32[4,320]{1,0:T(4,128)} copy(f32[4,320]{1,0:T(4,128)S(1)} %shard_map.82) | data formatting | bytes 10240

commit v6 on v5

--- a/solution.py
+++ b/solution.py
@@ -296,12 +296,18 @@
     inner_rows((0, span_y - 2))
     land(2, (0, 1))
     theirs = [weights(near_place.at[1 - k]) for k in (0, 1)]
-    land(0, range(6))
+    land(0, (0, 1))
     turn(0, edge[0, :, 0])
     turn(span_x + 1, edge[1, :, 0])
-    for x, a in ((0, 0), (span_x - 1, 2)):
-        for y in range(0, span_y, 2):
-            finish(x, y, early[x, y] + product(x, y, a, a + 1))
+
+    def outer_rows(some):
+        for y in some:
+            for x, a in ((0, 0), (span_x - 1, 2)):
+                finish(x, y, early[x, y] + product(x, y, a, a + 1))
+
+    outer_rows(range(2, span_y - 2, 2))
+    land(0, range(2, 6))
+    outer_rows((0, span_y - 2))
     start(1, range(2, 8))
 
     def sample(of_weights, x, weight, low, high):

time: 21.8 us -> 21.4 us (0.982)
  Pallas kernels: 21 us -> 20.7 us
    pallas_call x1, Pallas kernels: 21 us -> 20.7 us  [on_device(): pl.pallas_call(functools.partial(kernel, bricks, sects, slabs), out_shape...]
where the time goes in v6:
time: 21.4 us; the launch traced here: 21.3 us
  Pallas kernels  20.7 us (97%)
  local copies, waits for them, and re-layouts  0.6 us (3%)
    pallas_call x1, Pallas kernels, on_device(): pl.pallas_call(functools.partial(kernel, bricks, sects, slabs), out_shape...  20.7 us
    unnamed x1, local copies, waits for them, and re-layouts  0.6 us

profile of v6, /device:TPU:0, one launch (start us, length us, event | category | flops | bytes accessed | tf_op | source)
XLA Modules:
  0.0 21.3 jit_solution(9838608519567552482)
XLA Ops:
  0.0 20.7 %shard_map.82 = f32[4,320]{1,0:T(4,128)S(1)} custom-call(bf16[64,4,8,128]{3,2,1,0:T(8,128)(2,1)} %geometry.1, bf16[1,3,3,3,64,64]{5,4,3,2,1,0:T(8,128)(2,1)} %kernels.1, f32[3,256]{1,0:T(4,128)} %place_in.1, bf16[64,256]{1,0:T(8,128)(2,1)} %bitcast.2, s32[1,256]{1,0:T(1,128)} %bitcast.3, bf16[2,128,512]{2,1,0:T(8,128)(2,1)} %first.1, ...), custom_call_target="tpu_custom_call" | custom-call | tf_op jit(solution)/shard_map/pallas_call | solution.py:425
  20.7 0.6 %copy.10 = f32[4,320]{1,0:T(4,128)} copy(f32[4,320]{1,0:T(4,128)S(1)} %shard_map.82) | data formatting | bytes 10240

commit v7 on v6

--- a/solution.py
+++ b/solution.py
@@ -163,13 +163,18 @@
             device_id_type=MESH,
         )
 
+    middle_c = channels // 2
+
     def halo_copy(phase, k):
         dx, dy = DIRECTIONS[k]
         if phase == 1 and dy == 0:
             return remote(partial.at[k], incoming.at[k], phase, k)
         if phase == 0 and dy == 0:
             row = pl.ds(span_x - 1 if dx == 1 else 0, 1)
-            return remote(geometry.at[:, row], edge.at[k], phase, k)
+            return remote(geometry.at[:middle_c, row], edge.at[k, :middle_c], phase, k)
+        if phase == 3:
+            row = pl.ds(span_x - 1 if dx == 1 else 0, 1)
+            return remote(geometry.at[middle_c:, row], edge.at[k, middle_c:], phase, k)
         if phase == 2:
             return remote(place, near_place.at[k], phase, k)
         buffer = (pad, lat)[phase]
@@ -200,13 +205,13 @@
             def _():
                 halo_copy(phase, k).wait_send()
 
-    def turn(x, source):
-        base = x * channels * span_y
-        wide[base:base + channels * span_y] = source.astype(jnp.float32).reshape(
-            channels * span_y, span_z
-        )
+    def turn(x, source, first_c=0):
+        size = source.shape[0]
+        base = (x * channels + first_c) * span_y
+        wide[base:base + size * span_y] = source.astype(jnp.float32).reshape(size * span_y, span_z)
         for y in range(span_y):
-            pad[x, y + 1] = wide[pl.ds(base + y, channels, stride=span_y), :].astype(jnp.bfloat16)
+            turned = wide[pl.ds(base + y, size, stride=span_y), :].astype(jnp.bfloat16)
+            pad[x, y + 1, first_c:first_c + size] = turned
 
     cells = lax.broadcasted_iota(jnp.int32, (span_z, count), 0).astype(jnp.float32) + 0.5
 
@@ -222,6 +227,7 @@
 
     pl.semaphore_wait(barrier, expected)
     start(0, (0, 1))
+    start(3, (0, 1))
     loads[0].wait()
     start(2, (0, 1))
     for x in row_order[:2]:
@@ -296,9 +302,10 @@
     inner_rows((0, span_y - 2))
     land(2, (0, 1))
     theirs = [weights(near_place.at[1 - k]) for k in (0, 1)]
-    land(0, (0, 1))
-    turn(0, edge[0, :, 0])
-    turn(span_x + 1, edge[1, :, 0])
+    for phase, first_c in ((0, 0), (3, middle_c)):
+        land(phase, (0, 1))
+        turn(0, edge[0, first_c:first_c + middle_c, 0], first_c)
+        turn(span_x + 1, edge[1, first_c:first_c + middle_c, 0], first_c)
 
     def outer_rows(some):
         for y in some:
@@ -392,6 +399,7 @@
     drain(0, range(8))
     drain(1, range(8))
     drain(2, (0, 1))
+    drain(3, (0, 1))
     for j in range(1, peers):
         value_copy(j).wait()
 
@@ -447,8 +455,8 @@
             pltpu.VMEM((2, 8, width), jnp.float32),
             pltpu.VMEM((peers, 8, width), jnp.float32),
             pltpu.SemaphoreType.DMA((8 + span_x,)),
-            pltpu.SemaphoreType.DMA((3, 8)),
-            pltpu.SemaphoreType.DMA((3, 8)),
+            pltpu.SemaphoreType.DMA((4, 8)),
+            pltpu.SemaphoreType.DMA((4, 8)),
             pltpu.SemaphoreType.DMA((peers,)),
             pltpu.SemaphoreType.DMA((peers,)),
         ],

time: 21.4 us -> 21.6 us (level)
  no operation moved by 1% of the time
where the time goes in v7:
time: 21.6 us; the launch traced here: 21.4 us
  Pallas kernels  20.8 us (96%)
  local copies, waits for them, and re-layouts  0.6 us (3%)
    pallas_call x1, Pallas kernels, on_device(): pl.pallas_call(functools.partial(kernel, bricks, sects, slabs), out_shape...  20.8 us
    unnamed x1, local copies, waits for them, and re-layouts  0.6 us

profile of v7, /device:TPU:0, one launch (start us, length us, event | category | flops | bytes accessed | tf_op | source)
XLA Modules:
  0.0 21.4 jit_solution(6079018517092426125)
XLA Ops:
  0.0 20.8 %shard_map.82 = f32[4,320]{1,0:T(4,128)S(1)} custom-call(bf16[64,4,8,128]{3,2,1,0:T(8,128)(2,1)} %geometry.1, bf16[1,3,3,3,64,64]{5,4,3,2,1,0:T(8,128)(2,1)} %kernels.1, f32[3,256]{1,0:T(4,128)} %place_in.1, bf16[64,256]{1,0:T(8,128)(2,1)} %bitcast.2, s32[1,256]{1,0:T(1,128)} %bitcast.3, bf16[2,128,512]{2,1,0:T(8,128)(2,1)} %first.1, ...), custom_call_target="tpu_custom_call" | custom-call | tf_op jit(solution)/shard_map/pallas_call | solution.py:433
  20.8 0.6 %copy.10 = f32[4,320]{1,0:T(4,128)} copy(f32[4,320]{1,0:T(4,128)S(1)} %shard_map.82) | data formatting | bytes 10240

commit v8 on v6

--- a/solution.py
+++ b/solution.py
@@ -224,106 +224,6 @@
     start(0, (0, 1))
     loads[0].wait()
     start(2, (0, 1))
-    for x in row_order[:2]:
-        row_loads[x].wait()
-        turn(x + 1, geo[:, x])
-    start(0, range(2, 6))
-    for x in row_order[2:]:
-        row_loads[x].wait()
-        turn(x + 1, geo[:, x])
-    start(0, (6, 7))
-
-    for k, (dx, dy) in enumerate(DIRECTIONS):
-        @pl.when(jnp.logical_not(inside(-dx, -dy)))
-        def _():
-            if dy != 0:
-                for buffer in (pad, lat):
-                    region = buffer.at[land_range(dx, span_x), land_range(dy, span_y)]
-                    region[...] = jnp.zeros(region.shape, jnp.bfloat16)
-            else:
-                edge[k] = jnp.zeros(edge.shape[1:], jnp.bfloat16)
-                near_place[k] = jnp.zeros(near_place.shape[1:], jnp.float32)
-                incoming[k] = jnp.zeros(incoming.shape[1:], jnp.bfloat16)
-
-    loads[2].wait()
-    for a in range(3):
-        for b in range(3):
-            for e in range(3):
-                tap = taps[0, a, b, e].astype(jnp.float32).T.astype(jnp.bfloat16)
-                low = (a * 3 + b) * channels
-                taps_t[e * channels:(e + 1) * channels, low:low + channels] = tap
-
-    lane = lax.broadcasted_iota(jnp.int32, (channels, span_z), 1)
-
-    def product(x, y, low, high):
-        near = jnp.concatenate(
-            [
-                jnp.concatenate(
-                    [pad[x + a, y + i:y + i + 3].reshape(3 * channels, span_z) for i in (0, 1)],
-                    axis=1,
-                )
-                for a in range(low, high)
-            ],
-            axis=0,
-        )
-        return dot(taps_t[:, low * 3 * channels:high * 3 * channels], near)
-
-    def finish(x, y, pair):
-        for i in (0, 1):
-            part = pair[:, i * span_z:(i + 1) * span_z]
-            left = pltpu.roll(part[:channels], 1, 1)
-            right = pltpu.roll(part[2 * channels:], span_z - 1, 1)
-            response = (
-                part[channels:2 * channels]
-                + jnp.where(lane == 0, 0.0, left)
-                + jnp.where(lane == span_z - 1, 0.0, right)
-            )
-            old = pad[x + 1, y + i + 1].astype(jnp.float32)
-            lat[x + 1, y + i + 1] = (old + gelu(response)).astype(jnp.bfloat16)
-
-    early = {}
-
-    def inner_rows(some):
-        for x in range(1, span_x - 1):
-            for y in some:
-                finish(x, y, product(x, y, 0, 3))
-        for x, low, high in ((0, 1, 3), (span_x - 1, 0, 2)):
-            for y in some:
-                early[x, y] = product(x, y, low, high)
-
-    inner_rows(range(2, span_y - 2, 2))
-    land(0, (6, 7))
-    inner_rows((0, span_y - 2))
-    land(2, (0, 1))
-    theirs = [weights(near_place.at[1 - k]) for k in (0, 1)]
-    land(0, (0, 1))
-    turn(0, edge[0, :, 0])
-    turn(span_x + 1, edge[1, :, 0])
-
-    def outer_rows(some):
-        for y in some:
-            for x, a in ((0, 0), (span_x - 1, 2)):
-                finish(x, y, early[x, y] + product(x, y, a, a + 1))
-
-    outer_rows(range(2, span_y - 2, 2))
-    land(0, range(2, 6))
-    outer_rows((0, span_y - 2))
-    start(1, range(2, 8))
-
-    def sample(of_weights, x, weight, low, high):
-        weight_y, weight_z = of_weights[1:]
-        part = dot(lat[x, low:high].reshape((high - low) * channels, span_z), weight_z)
-        inner = None
-        for y in range(low, high):
-            term = part[(y - low) * channels:(y - low + 1) * channels] * weight_y[y]
-            inner = term if inner is None else inner + term
-        return inner * weight
-
-    for k, x, weight in ((0, span_x, 0), (1, 1, span_x + 1)):
-        weight_x = theirs[k][0][weight]
-        partial[k] = sample(theirs[k], x, weight_x, 1, span_y + 1).astype(jnp.bfloat16)
-        start(1, (k,))
-
     own_weights = weights(place)
 
     loads[1].wait()
@@ -343,6 +243,105 @@
     slots = lax.broadcasted_iota(jnp.int32, (2 * half, count), 0)
     gather = (slots == position.astype(jnp.int32)).astype(jnp.bfloat16)
 
+    for x in row_order[:2]:
+        row_loads[x].wait()
+        turn(x + 1, geo[:, x])
+    start(0, range(2, 6))
+    for x in row_order[2:]:
+        row_loads[x].wait()
+        turn(x + 1, geo[:, x])
+    start(0, (6, 7))
+
+    for k, (dx, dy) in enumerate(DIRECTIONS):
+        @pl.when(jnp.logical_not(inside(-dx, -dy)))
+        def _():
+            if dy != 0:
+                for buffer in (pad, lat):
+                    region = buffer.at[land_range(dx, span_x), land_range(dy, span_y)]
+                    region[...] = jnp.zeros(region.shape, jnp.bfloat16)
+            else:
+                edge[k] = jnp.zeros(edge.shape[1:], jnp.bfloat16)
+                near_place[k] = jnp.zeros(near_place.shape[1:], jnp.float32)
+                incoming[k] = jnp.zeros(incoming.shape[1:], jnp.bfloat16)
+
+    loads[2].wait()
+    for a in range(3):
+        for b in range(3):
+            for e in range(3):
+                tap = taps[0, a, b, e].astype(jnp.float32).T.astype(jnp.bfloat16)
+                low = (a * 3 + b) * channels
+                taps_t[e * channels:(e + 1) * channels, low:low + channels] = tap
+
+    lane = lax.broadcasted_iota(jnp.int32, (channels, span_z), 1)
+
+    def product(x, y, low, high):
+        near = jnp.concatenate(
+            [
+                jnp.concatenate(
+                    [pad[x + a, y + i:y + i + 3].reshape(3 * channels, span_z) for i in (0, 1)],
+                    axis=1,
+                )
+                for a in range(low, high)
+            ],
+            axis=0,
+        )
+        return dot(taps_t[:, low * 3 * channels:high * 3 * channels], near)
+
+    def finish(x, y, pair):
+        for i in (0, 1):
+            part = pair[:, i * span_z:(i + 1) * span_z]
+            left = pltpu.roll(part[:channels], 1, 1)
+            right = pltpu.roll(part[2 * channels:], span_z - 1, 1)
+            response = (
+                part[channels:2 * channels]
+                + jnp.where(lane == 0, 0.0, left)
+                + jnp.where(lane == span_z - 1, 0.0, right)
+            )
+            old = pad[x + 1, y + i + 1].astype(jnp.float32)
+            lat[x + 1, y + i + 1] = (old + gelu(response)).astype(jnp.bfloat16)
+
+    early = {}
+
+    def inner_rows(some):
+        for x in range(1, span_x - 1):
+            for y in some:
+                finish(x, y, product(x, y, 0, 3))
+        for x, low, high in ((0, 1, 3), (span_x - 1, 0, 2)):
+            for y in some:
+                early[x, y] = product(x, y, low, high)
+
+    inner_rows(range(2, span_y - 2, 2))
+    land(0, (6, 7))
+    inner_rows((0, span_y - 2))
+    land(2, (0, 1))
+    theirs = [weights(near_place.at[1 - k]) for k in (0, 1)]
+    land(0, (0, 1))
+    turn(0, edge[0, :, 0])
+    turn(span_x + 1, edge[1, :, 0])
+
+    def outer_rows(some):
+        for y in some:
+            for x, a in ((0, 0), (span_x - 1, 2)):
+                finish(x, y, early[x, y] + product(x, y, a, a + 1))
+
+    outer_rows(range(2, span_y - 2, 2))
+    land(0, range(2, 6))
+    outer_rows((0, span_y - 2))
+    start(1, range(2, 8))
+
+    def sample(of_weights, x, weight, low, high):
+        weight_y, weight_z = of_weights[1:]
+        part = dot(lat[x, low:high].reshape((high - low) * channels, span_z), weight_z)
+        inner = None
+        for y in range(low, high):
+            term = part[(y - low) * channels:(y - low + 1) * channels] * weight_y[y]
+            inner = term if inner is None else inner + term
+        return inner * weight
+
+    for k, x, weight in ((0, span_x, 0), (1, 1, span_x + 1)):
+        weight_x = theirs[k][0][weight]
+        partial[k] = sample(theirs[k], x, weight_x, 1, span_y + 1).astype(jnp.bfloat16)
+        start(1, (k,))
 
     outbox[...] = jnp.zeros(outbox.shape, jnp.float32)
     weight_x, weight_y, weight_z = own_weights

time: 21.4 us -> 21.4 us (level)
  no operation moved by 1% of the time
where the time goes in v8:
time: 21.4 us; the launch traced here: 21.3 us
  Pallas kernels  20.7 us (97%)
  local copies, waits for them, and re-layouts  0.6 us (3%)
    pallas_call x1, Pallas kernels, on_device(): pl.pallas_call(functools.partial(kernel, bricks, sects, slabs), out_shape...  20.7 us
    unnamed x1, local copies, waits for them, and re-layouts  0.6 us

profile of v8, /device:TPU:0, one launch (start us, length us, event | category | flops | bytes accessed | tf_op | source)
XLA Modules:
  0.0 21.3 jit_solution(11697332618004606684)
XLA Ops:
  0.0 20.7 %shard_map.82 = f32[4,320]{1,0:T(4,128)S(1)} custom-call(bf16[64,4,8,128]{3,2,1,0:T(8,128)(2,1)} %geometry.1, bf16[1,3,3,3,64,64]{5,4,3,2,1,0:T(8,128)(2,1)} %kernels.1, f32[3,256]{1,0:T(4,128)} %place_in.1, bf16[64,256]{1,0:T(8,128)(2,1)} %bitcast.2, s32[1,256]{1,0:T(1,128)} %bitcast.3, bf16[2,128,512]{2,1,0:T(8,128)(2,1)} %first.1, ...), custom_call_target="tpu_custom_call" | custom-call | tf_op jit(solution)/shard_map/pallas_call | solution.py:424
  20.7 0.6 %copy.10 = f32[4,320]{1,0:T(4,128)} copy(f32[4,320]{1,0:T(4,128)S(1)} %shard_map.82) | data formatting | bytes 10240
